TPU v7x, 512 devices: a whole 4x8x8 slice. The times are simulated.
512 devices in a mesh: dp: 32 (over y, x), fsdp: 16 (over z, core).
Axes of the slice: x: 4, y: 8, z: 8, core: 2. Of those that a mesh axis runs over, the one named last changes fastest.
Arguments:
- layer_input: bfloat16 [65536, 8192], P(('dp', 'fsdp')), may hold values from -24 to 24
- norm_gain: float32 [8192], P('fsdp'), may hold values from 0.4 to 2.4
- value_weight: bfloat16 [8192, 512], P('fsdp'), may hold values from -0.25 to 0.25
- value_cotangent: bfloat16 [65536, 512], P(('dp', 'fsdp')), may hold values from -36 to 36
Outputs:
- input_grad: bfloat16 [65536, 8192], P(('dp', 'fsdp'))
- weight_update: bfloat16 [8192, 512], P('fsdp', 'dp')
- gain_update: bfloat16 [8192], P('fsdp')
All inputs are finite; a program needn't handle non-finite values.
Results may differ from a plain program's by a relative error of at most 0.015.
Values may be sent and summed in bfloat16 or wider, within the bound.
No kernel may reach another device: no remote copies, remote signals or barrier semaphores. Data moves between devices by JAX's collectives and lax.ppermute only.
A program may use at most 64 MiB of HBM per device.

v0:
```python
import math

import jax
import jax.numpy as jnp
from jax import lax
from jax.sharding import PartitionSpec as P

EPS_NORM = 1e-05
EPS_SUM = 1e-06


def partner(block, axis, stride):
    count = lax.axis_size(axis)
    route = []
    for low in range(count):
        high = low | 1 << stride
        if high != low and high < count:
            route += [(low, high), (high, low)]
    return lax.ppermute(block, axis, route)


def combine_pair(mine, other, norm_mine, norm_other, inner):
    coef_mine = 1.0 - inner / (2.0 * (norm_mine + EPS_SUM))
    coef_other = 1.0 - inner / (2.0 * (norm_other + EPS_SUM))
    return (coef_mine * mine + coef_other * other).astype(jnp.bfloat16)


def body(layer_input, norm_gain, value_weight, value_cotangent):
    input32 = layer_input.astype(jnp.float32)
    inverse_rms = lax.rsqrt(jnp.mean(input32 * input32, axis=1, keepdims=True) + EPS_NORM)
    normed = input32 * inverse_rms
    normed_b = normed.astype(jnp.bfloat16)
    columns = lax.all_to_all(normed_b, "fsdp", split_axis=1, concat_axis=0, tiled=True)
    cotangent = lax.all_gather(value_cotangent, "fsdp", axis=0, tiled=True)
    grad_scale = 1.0 / math.sqrt(cotangent.shape[0])
    columns32 = columns.astype(jnp.float32)
    scaled = (columns32 * norm_gain[None, :]).astype(jnp.bfloat16)
    grad_w = (
        lax.dot_general(
            scaled, cotangent, (((0,), (0,)), ((), ())), preferred_element_type=jnp.float32
        )
        * grad_scale
    ).astype(jnp.bfloat16)
    back = lax.dot_general(
        cotangent, value_weight, (((1,), (1,)), ((), ())), preferred_element_type=jnp.float32
    )
    grad_g = (jnp.sum(back * columns32, axis=0) * grad_scale).astype(jnp.bfloat16)
    hat_grad = (back * norm_gain[None, :]).astype(jnp.bfloat16)
    returned = lax.all_to_all(hat_grad, "fsdp", split_axis=0, concat_axis=1, tiled=True)
    hat32 = returned.astype(jnp.float32)
    mean_term = jnp.mean(hat32 * normed, axis=1, keepdims=True)
    input_grad = (inverse_rms * (hat32 - normed * mean_term)).astype(jnp.bfloat16)
    levels = lax.axis_size("dp").bit_length() - 1
    replica = lax.axis_index("dp")
    mine_w, mine_g = (grad_w, grad_g)
    for depth_step in range(levels):
        pair_bit = levels - 1 - depth_step
        other_w, other_g = partner((mine_w, mine_g), "dp", pair_bit)
        first_w = mine_w.astype(jnp.float32)
        second_w = other_w.astype(jnp.float32)
        first_g = mine_g.astype(jnp.float32)
        second_g = other_g.astype(jnp.float32)
        totals = lax.psum(
            (
                jnp.sum(first_w * first_w),
                jnp.sum(second_w * second_w),
                jnp.sum(first_w * second_w),
                jnp.sum(first_g * first_g),
                jnp.sum(second_g * second_g),
                jnp.sum(first_g * second_g),
            ),
            "fsdp",
        )
        mine_w = combine_pair(first_w, second_w, totals[0], totals[1], totals[2])
        mine_g = combine_pair(first_g, second_g, totals[3], totals[4], totals[5])
    width_own = mine_w.shape[1] // lax.axis_size("dp")
    weight_update = lax.dynamic_slice_in_dim(mine_w, replica * width_own, width_own, 1)
    return (input_grad, weight_update, mine_g)


def solution(mesh):
    in_specs = (P(("dp", "fsdp"), None), P("fsdp"), P("fsdp", None), P(("dp", "fsdp"), None))
    out_specs = (P(("dp", "fsdp"), None), P("fsdp", "dp"), P("fsdp"))
    return jax.shard_map(body, mesh=mesh, in_specs=in_specs, out_specs=out_specs, check_vma=False)
```

profile of v0, /device:TPU:1, one launch (start us, length us, event | category | flops | bytes accessed | tf_op | source)
XLA Modules:
  0.0 394.1 jit_solution(2813276321227927210)
XLA Ops:
  7.2 0.7 all-gather.2.cloned.1.call-update
  7.9 2.1 fusion.7
  10.5 1.5 copy.12
  12.0 12.0 %all-to-all-start.1 = ((bf16[128,16,512]{2,0,1:T(8,128)(2,1)}), bf16[128,16,512]{2,0,1:T(8,128)(2,1)}, u32[]{:S(2)}, u32[]{:S(2)}) async-start(bf16[128,16,512]{2,0,1:T(8,128)(2,1)} %bitcast.24), calls=%async_computation.1 | async-start | bytes 4194304 | tf_op jit(solution)/shard_map/all_to_all | solution.py:33
  24.0 58.5 %all-gather.2.cloned.1.call-done = bf16[2048,512]{1,0:T(8,128)(2,1)} async-done(((bf16[128,512]{1,0:T(8,128)(2,1)}), bf16[2048,512]{1,0:T(8,128)(2,1)}) %all-gather.2.cloned.1.call-update) | async-done | bytes 2097168 | tf_op jit(solution)/shard_map/all_gather | solution.py:34
  82.5 5.3 %fusion.9 = (f32[512]{0:T(512)S(1)}, bf16[2048,512]{1,0:T(8,128)(2,1)}, bf16[2048,512]{1,0:T(8,128)(2,1)S(1)}) fusion(bf16[128,16,512]{2,0,1:T(8,128)(2,1)} %all-to-all-done.1, f32[512]{0:T(512)S(1)} %copy-done.6, bf16[2048,512]{1,0:T(8,128)(2,1)} %all-gather.2.cloned.1.call-done, bf16[512,512]{1,0:T(8,128)(2,1)S(1)} %copy-done), kind=kOutput, calls=%fused_computation.13 | convolution fusion | flops 1081081344 | bytes 8916992 | tf_op jit(solution)/shard_map/dot_general | solution.py:44
  87.8 1.3 fusion.10
  89.1 7.3 %collective-permute-start = (bf16[512,512]{0,1:T(8,128)(2,1)S(1)}, bf16[512,512]{0,1:T(8,128)(2,1)S(1)}, u32[]{:S(2)}, u32[]{:S(2)}) collective-permute-start(bf16[512,512]{0,1:T(8,128)(2,1)S(1)} %fusion.10), channel_id=1, source_target_pairs={{0,256},{256,0},{16,272},{272,16},{32,288},{288,32},{48,304},{304,... | collective-permute-start | bytes 1572872 | tf_op jit(solution)/shard_map/ppermute | solution.py:19
  96.5 1.9 collective-permute-start.5
  98.4 12.6 %collective-permute-done.5 = bf16[512]{0:T(512)(128)(2,1)S(1)} collective-permute-done((bf16[512]{0:T(512)(128)(2,1)S(1)}, bf16[512]{0:T(512)(128)(2,1)S(1)}, u32[]{:S(2)}, u32[]{:S(2)}) %collective-permute-start.5) | collective-permute-done | bytes 1056 | tf_op jit(solution)/shard_map/ppermute | solution.py:19
  111.0 0.7 fusion.33
  111.7 1.0 fusion.11
  112.7 32.5 %all-reduce.4 = (f32[]{:T(128)}, f32[]{:T(128)}, f32[]{:T(128)}, f32[]{:T(128)}, f32[]{:T(128)}, /*index=5*/f32[]{:T(128)}) all-reduce(f32[]{:T(128)} %get-tuple-element.16, f32[]{:T(128)} %get-tuple-element.17, f32[]{:T(128)} %get-tuple-element.15, f32[]{:T(128)} %get-tuple-element.31, ...), channel_id=1, replica_groups=mesh['dp'=32,'fsdp'=16] {'fsdp'}, use_global_device_ids=true, to_apply=%region_3.0 | all-reduce | flops 6 | bytes 48 | tf_op jit(solution)/shard_map/psum | solution.py:63
  147.8 1.4 fusion.13
  149.2 4.8 %collective-permute-start.1 = (bf16[512,512]{0,1:T(8,128)(2,1)S(1)}, bf16[512,512]{0,1:T(8,128)(2,1)}, u32[]{:S(2)}, u32[]{:S(2)}) collective-permute-start(bf16[512,512]{0,1:T(8,128)(2,1)S(1)} %fusion.13), channel_id=1, source_target_pairs={{0,128},{128,0},{16,144},{144,16},{32,160},{160,32},{48,176},{176,... | collective-permute-start | bytes 1572872 | tf_op jit(solution)/shard_map/ppermute | solution.py:19
  154.0 10.3 %all-to-all-start = ((bf16[16,128,512]{2,1,0:T(8,128)(2,1)}), bf16[16,128,512]{2,1,0:T(8,128)(2,1)}, u32[]{:S(2)}, u32[]{:S(2)}) async-start(bf16[16,128,512]{2,1,0:T(8,128)(2,1)} %bitcast.26), calls=%async_computation | async-start | bytes 4194304 | tf_op jit(solution)/shard_map/all_to_all | solution.py:49
  166.8 1.9 collective-permute-start.6
  168.7 8.2 %collective-permute-done.6 = bf16[512]{0:T(512)(128)(2,1)S(1)} collective-permute-done((bf16[512]{0:T(512)(128)(2,1)S(1)}, bf16[512]{0:T(512)(128)(2,1)S(1)}, u32[]{:S(2)}, u32[]{:S(2)}) %collective-permute-start.6) | collective-permute-done | bytes 1056 | tf_op jit(solution)/shard_map/ppermute | solution.py:19
  176.8 0.7 fusion.38
  177.5 1.9 fusion.16
  179.4 51.7 %all-reduce.3 = (f32[]{:T(128)}, f32[]{:T(128)}, f32[]{:T(128)}, f32[]{:T(128)}, f32[]{:T(128)}, /*index=5*/f32[]{:T(128)}) all-reduce(f32[]{:T(128)} %get-tuple-element.13, f32[]{:T(128)} %get-tuple-element.14, f32[]{:T(128)} %get-tuple-element.12, f32[]{:T(128)} %get-tuple-element.28, ...), channel_id=1, replica_groups=mesh['dp'=32,'fsdp'=16] {'fsdp'}, use_global_device_ids=true, to_apply=%region_9.0 | all-reduce | flops 6 | bytes 48 | tf_op jit(solution)/shard_map/psum | solution.py:63
  233.8 2.0 fusion.18
  235.8 1.9 collective-permute-start.2
  240.2 3.4 collective-permute-start.7
  243.5 6.7 %collective-permute-done.7 = bf16[512]{0:T(512)(128)(2,1)S(1)} collective-permute-done((bf16[512]{0:T(512)(128)(2,1)S(1)}, bf16[512]{0:T(512)(128)(2,1)S(1)}, u32[]{:S(2)}, u32[]{:S(2)}) %collective-permute-start.7) | collective-permute-done | bytes 1056 | tf_op jit(solution)/shard_map/ppermute | solution.py:19
  250.2 0.7 fusion.43
  250.9 2.1 fusion.21
  253.1 25.7 %all-reduce.2 = (f32[]{:T(128)}, f32[]{:T(128)}, f32[]{:T(128)}, f32[]{:T(128)}, f32[]{:T(128)}, /*index=5*/f32[]{:T(128)}) all-reduce(f32[]{:T(128)} %get-tuple-element.10, f32[]{:T(128)} %get-tuple-element.11, f32[]{:T(128)} %get-tuple-element.9, f32[]{:T(128)} %get-tuple-element.25, ...), channel_id=1, replica_groups=mesh['dp'=32,'fsdp'=16] {'fsdp'}, use_global_device_ids=true, to_apply=%region_15.0 | all-reduce | flops 6 | bytes 48 | tf_op jit(solution)/shard_map/psum | solution.py:63
  281.3 1.4 fusion.23
  282.7 3.5 collective-permute-start.3
  288.6 3.3 collective-permute-start.8
  291.9 7.1 %collective-permute-done.8 = bf16[512]{0:T(512)(128)(2,1)S(1)} collective-permute-done((bf16[512]{0:T(512)(128)(2,1)S(1)}, bf16[512]{0:T(512)(128)(2,1)S(1)}, u32[]{:S(2)}, u32[]{:S(2)}) %collective-permute-start.8) | collective-permute-done | bytes 1056 | tf_op jit(solution)/shard_map/ppermute | solution.py:19
  299.0 0.7 fusion.48
  299.7 1.9 fusion.26
  301.6 25.1 %all-reduce.1 = (f32[]{:T(128)}, f32[]{:T(128)}, f32[]{:T(128)}, f32[]{:T(128)}, f32[]{:T(128)}, /*index=5*/f32[]{:T(128)}) all-reduce(f32[]{:T(128)} %get-tuple-element.7, f32[]{:T(128)} %get-tuple-element.8, f32[]{:T(128)} %get-tuple-element.6, f32[]{:T(128)} %get-tuple-element.22, ...), channel_id=1, replica_groups=mesh['dp'=32,'fsdp'=16] {'fsdp'}, use_global_device_ids=true, to_apply=%region_21.0 | all-reduce | flops 6 | bytes 48 | tf_op jit(solution)/shard_map/psum | solution.py:63
  329.3 2.4 fusion.58
  331.7 2.4 collective-permute-start.4
  336.7 2.9 collective-permute-start.9
  339.6 7.1 %collective-permute-done.9 = bf16[512]{0:T(512)(128)(2,1)S(1)} collective-permute-done((bf16[512]{0:T(512)(128)(2,1)S(1)}, bf16[512]{0:T(512)(128)(2,1)S(1)}, u32[]{:S(2)}, u32[]{:S(2)}) %collective-permute-start.9) | collective-permute-done | bytes 1056 | tf_op jit(solution)/shard_map/ppermute | solution.py:19
  346.7 0.7 fusion.53
  347.3 1.9 multiply_reduce_fusion.1
  349.3 25.2 %all-reduce = (f32[]{:T(128)}, f32[]{:T(128)}, f32[]{:T(128)}, f32[]{:T(128)}, f32[]{:T(128)}, /*index=5*/f32[]{:T(128)}) all-reduce(f32[]{:T(128)} %get-tuple-element.4, f32[]{:T(128)} %get-tuple-element.5, f32[]{:T(128)} %get-tuple-element.3, f32[]{:T(128)} %get-tuple-element.19, ...), channel_id=1, replica_groups=mesh['dp'=32,'fsdp'=16] {'fsdp'}, use_global_device_ids=true, to_apply=%region_27.0 | all-reduce | flops 6 | bytes 48 | tf_op jit(solution)/shard_map/psum | solution.py:63
  379.6 1.4 fusion.32
  381.0 0.6 fusion.55
  381.6 2.1 convert_bitcast_fusion
  383.8 0.5 copy.10
  384.2 0.8 fusion.3
  385.0 2.3 fusion.6
  (31 shorter events, 0.7 us)
Async XLA Ops:
  7.2 75.4 %copy-start = (bf16[512,512]{1,0:T(8,128)(2,1)S(1)}, bf16[512,512]{1,0:T(8,128)(2,1)}, u32[]{:S(2)}) copy-start(bf16[512,512]{1,0:T(8,128)(2,1)} %param.6) | copy-start | bytes 1572868
  7.2 2.8 copy-start.1
  7.2 75.3 %all-gather.2.cloned.1.call-start = ((), (), s32[]{:S(2)}) async-start(), calls=%async_computation.2 | async-start | bytes 2228224 | tf_op jit(solution)/shard_map/all_gather | solution.py:34
  12.0 70.5 %copy-start.6 = (f32[512]{0:T(512)S(1)}, f32[512]{0:T(512)}, u32[]{:S(2)}) copy-start(f32[512]{0:T(512)} %param.5) | copy-start | bytes 6148
  12.0 70.5 %all-to-all-start.1 = ((bf16[128,16,512]{2,0,1:T(8,128)(2,1)}), bf16[128,16,512]{2,0,1:T(8,128)(2,1)}, u32[]{:S(2)}, u32[]{:S(2)}) async-start(bf16[128,16,512]{2,0,1:T(8,128)(2,1)} %bitcast.24), calls=%async_computation.1 | async-start | bytes 4194304 | tf_op jit(solution)/shard_map/all_to_all | solution.py:33
  82.5 5.3 %copy-start.5 = (bf16[2048,512]{1,0:T(8,128)(2,1)S(1)}, bf16[2048,512]{1,0:T(8,128)(2,1)}, u32[]{:S(2)}) copy-start(bf16[2048,512]{1,0:T(8,128)(2,1)} %all-gather.2.cloned.1.call-done) | copy-start | bytes 6291460
  89.1 22.6 %copy-start.3 = (bf16[512,512]{0,1:T(8,128)(2,1)}, bf16[512,512]{0,1:T(8,128)(2,1)S(1)}, u32[]{:S(2)}) copy-start(bf16[512,512]{0,1:T(8,128)(2,1)S(1)} %fusion.10) | copy-start | bytes 1572868
  89.1 22.6 %collective-permute-start = (bf16[512,512]{0,1:T(8,128)(2,1)S(1)}, bf16[512,512]{0,1:T(8,128)(2,1)S(1)}, u32[]{:S(2)}, u32[]{:S(2)}) collective-permute-start(bf16[512,512]{0,1:T(8,128)(2,1)S(1)} %fusion.10), channel_id=1, source_target_pairs={{0,256},{256,0},{16,272},{272,16},{32,288},{288,32},{48,304},{304,... | collective-permute-start | bytes 1572872 | tf_op jit(solution)/shard_map/ppermute | solution.py:19
  96.5 14.5 %collective-permute-start.5 = (bf16[512]{0:T(512)(128)(2,1)S(1)}, bf16[512]{0:T(512)(128)(2,1)S(1)}, u32[]{:S(2)}, u32[]{:S(2)}) collective-permute-start(bf16[512]{0:T(512)(128)(2,1)S(1)} %multiply_convert_fusion.1), channel_id=1, source_target_pairs={{0,256},{256,0},{16,272},{272,16},{32,288},{288,32},{48,304},{304,... | collective-permute-start | bytes 3080 | tf_op jit(solution)/shard_map/ppermute | solution.py:19
  111.7 1.0 copy-start.4
  149.2 28.3 %collective-permute-start.1 = (bf16[512,512]{0,1:T(8,128)(2,1)S(1)}, bf16[512,512]{0,1:T(8,128)(2,1)}, u32[]{:S(2)}, u32[]{:S(2)}) collective-permute-start(bf16[512,512]{0,1:T(8,128)(2,1)S(1)} %fusion.13), channel_id=1, source_target_pairs={{0,128},{128,0},{16,144},{144,16},{32,160},{160,32},{48,176},{176,... | collective-permute-start | bytes 1572872 | tf_op jit(solution)/shard_map/ppermute | solution.py:19
  154.0 227.6 %all-to-all-start = ((bf16[16,128,512]{2,1,0:T(8,128)(2,1)}), bf16[16,128,512]{2,1,0:T(8,128)(2,1)}, u32[]{:S(2)}, u32[]{:S(2)}) async-start(bf16[16,128,512]{2,1,0:T(8,128)(2,1)} %bitcast.26), calls=%async_computation | async-start | bytes 4194304 | tf_op jit(solution)/shard_map/all_to_all | solution.py:49
  166.8 10.1 %collective-permute-start.6 = (bf16[512]{0:T(512)(128)(2,1)S(1)}, bf16[512]{0:T(512)(128)(2,1)S(1)}, u32[]{:S(2)}, u32[]{:S(2)}) collective-permute-start(bf16[512]{0:T(512)(128)(2,1)S(1)} %fusion.35), channel_id=1, source_target_pairs={{0,128},{128,0},{16,144},{144,16},{32,160},{160,32},{48,176},{176,... | collective-permute-start | bytes 3080 | tf_op jit(solution)/shard_map/ppermute | solution.py:19
  235.8 15.1 %collective-permute-start.2 = (bf16[512,512]{0,1:T(8,128)(2,1)}, bf16[512,512]{0,1:T(8,128)(2,1)S(1)}, u32[]{:S(2)}, u32[]{:S(2)}) collective-permute-start(bf16[512,512]{0,1:T(8,128)(2,1)} %fusion.18), channel_id=1, source_target_pairs={{0,64},{64,0},{16,80},{80,16},{32,96},{96,32},{48,112},{112,48},{1... | collective-permute-start | bytes 1572872 | tf_op jit(solution)/shard_map/ppermute | solution.py:19
  240.2 10.1 %collective-permute-start.7 = (bf16[512]{0:T(512)(128)(2,1)S(1)}, bf16[512]{0:T(512)(128)(2,1)S(1)}, u32[]{:S(2)}, u32[]{:S(2)}) collective-permute-start(bf16[512]{0:T(512)(128)(2,1)S(1)} %fusion.40), channel_id=1, source_target_pairs={{0,64},{64,0},{16,80},{80,16},{32,96},{96,32},{48,112},{112,48},{1... | collective-permute-start | bytes 3080 | tf_op jit(solution)/shard_map/ppermute | solution.py:19
  250.9 30.3 %copy-start.2 = (bf16[512,512]{0,1:T(8,128)(2,1)}, bf16[512,512]{0,1:T(8,128)(2,1)S(1)}, u32[]{:S(2)}) copy-start(bf16[512,512]{0,1:T(8,128)(2,1)S(1)} %collective-permute-done.2) | copy-start | bytes 1572868
  282.7 17.0 %collective-permute-start.3 = (bf16[512,512]{0,1:T(8,128)(2,1)S(1)}, bf16[512,512]{0,1:T(8,128)(2,1)}, u32[]{:S(2)}, u32[]{:S(2)}) collective-permute-start(bf16[512,512]{0,1:T(8,128)(2,1)S(1)} %fusion.23), channel_id=1, source_target_pairs={{0,32},{32,0},{16,48},{48,16},{64,96},{96,64},{80,112},{112,80},{1... | collective-permute-start | bytes 1572872 | tf_op jit(solution)/shard_map/ppermute | solution.py:19
  288.6 10.4 %collective-permute-start.8 = (bf16[512]{0:T(512)(128)(2,1)S(1)}, bf16[512]{0:T(512)(128)(2,1)S(1)}, u32[]{:S(2)}, u32[]{:S(2)}) collective-permute-start(bf16[512]{0:T(512)(128)(2,1)S(1)} %fusion.45), channel_id=1, source_target_pairs={{0,32},{32,0},{16,48},{48,16},{64,96},{96,64},{80,112},{112,80},{1... | collective-permute-start | bytes 3080 | tf_op jit(solution)/shard_map/ppermute | solution.py:19
  331.7 15.6 %collective-permute-start.4 = (bf16[512,512]{0,1:T(8,128)(2,1)}, bf16[512,512]{0,1:T(8,128)(2,1)S(1)}, u32[]{:S(2)}, u32[]{:S(2)}) collective-permute-start(bf16[512,512]{0,1:T(8,128)(2,1)} %get-tuple-element.64), channel_id=1, source_target_pairs={{0,16},{16,0},{32,48},{48,32},{64,80},{80,64},{96,112},{112,96},{1... | collective-permute-start | bytes 1572872 | tf_op jit(solution)/shard_map/ppermute | solution.py:19
  336.7 10.0 %collective-permute-start.9 = (bf16[512]{0:T(512)(128)(2,1)S(1)}, bf16[512]{0:T(512)(128)(2,1)S(1)}, u32[]{:S(2)}, u32[]{:S(2)}) collective-permute-start(bf16[512]{0:T(512)(128)(2,1)S(1)} %fusion.50), channel_id=1, source_target_pairs={{0,16},{16,0},{32,48},{48,32},{64,80},{80,64},{96,112},{112,96},{1... | collective-permute-start | bytes 3080 | tf_op jit(solution)/shard_map/ppermute | solution.py:19
Sparse Core Ops, SparseCore 0:
  10.1 72.3 all-gather.1
where the time goes:
time: 396 us; the launch traced here: 394 us
  blocking collectives  160 us (40%)
  waiting for transfers between devices  101 us (26%)
  starting transfers between devices  55.6 us (14%)
  between operations  39.5 us (10%)
  other arithmetic  29.4 us (7%)
  matrix products  6.57 us (2%)
    psum x5, blocking collectives, body(): lax.psum((jnp.sum(first_w * first_w), jnp.sum(second_w * second_w), jnp.s...  160 us
    all_gather x1, waiting for transfers between devices, body(): cotangent = lax.all_gather(value_cotangent, 'fsdp', axis=0, tiled=True)  58.5 us
    ppermute x10, waiting for transfers between devices, partner(): return lax.ppermute(block, axis, route)  41.6 us
    ppermute x10, starting transfers between devices, partner(): return lax.ppermute(block, axis, route)  33.3 us
    all_to_all x1, starting transfers between devices, body(): lax.all_to_all(normed_b, 'fsdp', split_axis=1, concat_axis=0, tiled=True)  12 us
    all_to_all x1, starting transfers between devices, body(): lax.all_to_all(hat_grad, 'fsdp', split_axis=0, concat_axis=1, tiled=True)  10.3 us
    reduce_sum x5, other arithmetic, body(): jnp.sum(first_w * first_w)  8.93 us
  transfers between devices with their start and end apart: 13, of which 6 were waited for; matrix products, arithmetic and copies ran while one was open for 6% of the time, Pallas kernels for 0%

commit v1 on v0

v1 whole, which is shorter than its diff:
```python
import math

import jax
import jax.numpy as jnp
from jax import lax
from jax.experimental import pallas as pl
from jax.experimental.pallas import tpu as pltpu
from jax.sharding import PartitionSpec as P

EPS_NORM = 1e-05
EPS_SUM = 1e-06
REPLICAS = 32
LANES = 128


def pack_gram(gram):
    row = lax.broadcasted_iota(jnp.int32, gram.shape, 0)
    lane = lax.broadcasted_iota(jnp.int32, gram.shape, 1)
    kept = jnp.where(row // 8 == lane // REPLICAS, gram, 0.0)
    return kept[0:8] + kept[8:16] + kept[16:24] + kept[24:32]


def unpack_gram(packed):
    tiled = jnp.concatenate([packed] * 4, axis=0)
    row = lax.broadcasted_iota(jnp.int32, tiled.shape, 0)
    lane = lax.broadcasted_iota(jnp.int32, tiled.shape, 1)
    kept = jnp.where(row // 8 == lane // REPLICAS, tiled, 0.0)
    kept = kept + pltpu.roll(kept, 64, 1)
    return kept + pltpu.roll(kept, 32, 1)


def gram_kernel(shards_ref, gain_ref, out_ref):
    shards = shards_ref[...]
    products = lax.dot_general(
        shards, shards, (((1,), (1,)), ((), ())), preferred_element_type=jnp.float32
    )
    rows, width = products.shape[0], shards.shape[0] // REPLICAS
    row = lax.broadcasted_iota(jnp.int32, products.shape, 0)
    column = lax.broadcasted_iota(jnp.int32, products.shape, 1)
    kept = jnp.where(row % width == column % width, products, 0.0)
    folded = jnp.sum(kept.reshape(REPLICAS, width, rows), axis=1)
    source = lax.broadcasted_iota(jnp.int32, (rows, LANES), 0)
    target = lax.broadcasted_iota(jnp.int32, (rows, LANES), 1)
    spread = jnp.where(source // width == target % REPLICAS, 1.0, 0.0)
    gram = jnp.dot(
        folded, spread, precision=lax.Precision.HIGHEST, preferred_element_type=jnp.float32
    )
    packed = pack_gram(gram)
    gain = gain_ref[...]
    for peer in range(out_ref.shape[0]):
        out_ref[peer, 0:8, :] = packed
        for part in range(4):
            out_ref[peer, 8 + part : 9 + part, :] = gain[:, part * LANES : (part + 1) * LANES]
        out_ref[peer, 12:16, :] = jnp.zeros((4, LANES), jnp.float32)


def gain_gram_kernel(parts_ref, out_ref):
    packed = jnp.sum(parts_ref[:, 0:8, :], axis=0)
    gram = jnp.zeros((REPLICAS, REPLICAS), jnp.float32)
    for part in range(4):
        piece = parts_ref[:, 8 + part, :].astype(jnp.bfloat16)
        gram += lax.dot_general(
            piece, piece, (((1,), (1,)), ((), ())), preferred_element_type=jnp.float32
        )
    packed_gain = pack_gram(jnp.concatenate([gram] * 4, axis=1))
    for peer in range(out_ref.shape[0]):
        out_ref[peer, 0:8, :] = packed
        out_ref[peer, 8:16, :] = packed_gain


def swap(values, stride, axis):
    size = values.shape[axis]
    index = lax.broadcasted_iota(jnp.int32, values.shape, axis)
    up = pltpu.roll(values, size - stride, axis)
    down = pltpu.roll(values, stride, axis)
    return jnp.where((index & stride) == 0, up, down)


def pair_weights(gram):
    row = lax.broadcasted_iota(jnp.int32, gram.shape, 0)
    lane = lax.broadcasted_iota(jnp.int32, gram.shape, 1)
    column = lane % REPLICAS
    first = lane < REPLICAS
    weights = jnp.ones((REPLICAS, 1), jnp.float32)
    for stride in (16, 8, 4, 2, 1):
        same = row == column
        met = row == (column ^ stride)

        def coefs(axis, only):
            norm = jnp.sum(jnp.where(same & only, gram, 0.0), axis=axis, keepdims=True)
            inner = jnp.sum(jnp.where(met & only, gram, 0.0), axis=axis, keepdims=True)
            return 1.0 - inner / (2.0 * (jnp.maximum(norm, 0.0) + EPS_SUM))

        down = coefs(1, first)
        weights = weights * down
        if stride > 1:
            scaled = gram * down * coefs(0, True)
            scaled = scaled + swap(scaled, stride, 0)
            gram = scaled + swap(scaled, stride, 1)
    return weights


def combine_kernel(packed_ref, shards_ref, parts_ref, weight_ref, gain_ref):
    packed = jnp.sum(packed_ref[...], axis=0)
    weights_w = pair_weights(unpack_gram(packed[0:8]))
    weights_g = pair_weights(unpack_gram(packed[8:16]))
    width = shards_ref.shape[0] // REPLICAS
    total = jnp.zeros((width, shards_ref.shape[1]), jnp.float32)
    for replica in range(REPLICAS):
        shard = shards_ref[replica * width : (replica + 1) * width, :].astype(jnp.float32)
        total += weights_w[replica : replica + 1, :] * shard
    weight_ref[...] = total.T.astype(jnp.bfloat16)
    for part in range(4):
        piece = parts_ref[:, 8 + part, :]
        gain_ref[:, part * LANES : (part + 1) * LANES] = jnp.sum(
            weights_g * piece, axis=0, keepdims=True
        ).astype(jnp.bfloat16)


def kernel_call(kernel, out_shape, *args):
    return pl.pallas_call(
        kernel,
        out_shape=out_shape,
        compiler_params=pltpu.CompilerParams(vmem_limit_bytes=32 * 1024 * 1024),
    )(*args)


def body(layer_input, norm_gain, value_weight, value_cotangent):
    tokens, model = layer_input.shape
    peers = lax.axis_size("fsdp")
    columns = lax.all_to_all(layer_input, "fsdp", split_axis=1, concat_axis=0, tiled=True)
    input32 = layer_input.astype(jnp.float32)
    inverse_rms = lax.rsqrt(jnp.mean(input32 * input32, axis=1, keepdims=True) + EPS_NORM)
    scaled_cotangent = (value_cotangent.astype(jnp.float32) * inverse_rms).astype(jnp.bfloat16)
    cotangent = lax.all_gather(scaled_cotangent, "fsdp", axis=0, tiled=True)
    grad_scale = 1.0 / math.sqrt(cotangent.shape[0])
    grad = lax.dot_general(
        cotangent, columns, (((0,), (0,)), ((), ())), preferred_element_type=jnp.float32
    )
    grad_w = (grad * (norm_gain * grad_scale)[None, :]).astype(jnp.bfloat16)
    weight_t = value_weight.T.astype(jnp.float32)
    grad_g = (jnp.sum(grad * weight_t, axis=0, keepdims=True) * grad_scale).astype(jnp.bfloat16)
    back = lax.dot_general(
        cotangent, value_weight, (((1,), (1,)), ((), ())), preferred_element_type=jnp.float32
    )
    hat_grad = (back * norm_gain[None, :]).astype(jnp.bfloat16)
    shards = lax.all_to_all(grad_w, "dp", split_axis=0, concat_axis=0, tiled=True)
    returned = lax.all_to_all(hat_grad, "fsdp", split_axis=0, concat_axis=1, tiled=True)

    sent = kernel_call(
        gram_kernel,
        jax.ShapeDtypeStruct((REPLICAS, 16, LANES), jnp.float32),
        shards,
        grad_g.astype(jnp.float32),
    )
    parts = lax.all_to_all(sent, "dp", split_axis=0, concat_axis=0, tiled=True)
    sent = kernel_call(
        gain_gram_kernel, jax.ShapeDtypeStruct((peers, 16, LANES), jnp.float32), parts
    )
    packed = lax.all_to_all(sent, "fsdp", split_axis=0, concat_axis=0, tiled=True)
    weight_update, gain_update = kernel_call(
        combine_kernel,
        (
            jax.ShapeDtypeStruct((shards.shape[1], shards.shape[0] // REPLICAS), jnp.bfloat16),
            jax.ShapeDtypeStruct((1, shards.shape[1]), jnp.bfloat16),
        ),
        packed,
        shards,
        parts,
    )
    hat32 = returned.astype(jnp.float32)
    mean_term = jnp.mean(hat32 * input32, axis=1, keepdims=True)
    input_grad = (hat32 - input32 * (inverse_rms * inverse_rms * mean_term)).astype(jnp.bfloat16)
    return (input_grad, weight_update, gain_update[0])


def solution(mesh):
    in_specs = (P(("dp", "fsdp"), None), P("fsdp"), P("fsdp", None), P(("dp", "fsdp"), None))
    out_specs = (P(("dp", "fsdp"), None), P("fsdp", "dp"), P("fsdp"))
    return jax.shard_map(body, mesh=mesh, in_specs=in_specs, out_specs=out_specs, check_vma=False)
```

time: 396 us -> 218 us (0.55)
  blocking collectives: 160 us -> 15.2 us
  between operations: 39.5 us -> 14.2 us
  waiting for transfers between devices: 101 us -> 126 us
  other arithmetic: 29.4 us -> 6.55 us
  starting transfers between devices: 55.6 us -> 34.7 us
  local copies, waits for them, and re-layouts: 2.06 us -> 9.71 us
    psum x5 -> x0, blocking collectives: 160 us -> none  [body(): lax.psum((jnp.sum(first_w * first_w), jnp.sum(second_w * second_w), jnp.s...]
    all_to_all x1 -> x3, waiting for transfers between devices: 0.01 us -> 76.4 us  [the longest x1 54.8 us: body(): lax.all_to_all(layer_input, 'fsdp', split_axis=1, concat_axis=0, tiled=True)]
    all_gather x1, waiting for transfers between devices: 58.5 us -> 3.79 us  [body(): cotangent = lax.all_gather(scaled_cotangent, 'fsdp', axis=0, tiled=True)]
    all_to_all x1, waiting for transfers between devices: 0.01 us -> 45.8 us  [body(): lax.all_to_all(hat_grad, 'fsdp', split_axis=0, concat_axis=1, tiled=True)]
    ppermute x10 -> x0, waiting for transfers between devices: 41.6 us -> none  [partner(): return lax.ppermute(block, axis, route)]
    ppermute x10 -> x0, starting transfers between devices: 33.3 us -> none  [partner(): return lax.ppermute(block, axis, route)]
    all_to_all x1 -> x3, starting transfers between devices: 12 us -> 30.3 us  [the longest x1 12 us: body(): lax.all_to_all(layer_input, 'fsdp', split_axis=1, concat_axis=0, tiled=True)]
    all_to_all x0 -> x1, blocking collectives: none -> 15.2 us  [body(): parts = lax.all_to_all(sent, 'dp', split_axis=0, concat_axis=0, tiled=True)]
  transfers between devices with their start and end apart: 13 -> 5, of which waited for: 6 -> 5; matrix products, arithmetic and copies ran while one was open for 6% -> 5% of each run, Pallas kernels for 0% -> 1%
where the time goes in v1:
time: 218 us
  waiting for transfers between devices  126 us (58%)
  starting transfers between devices  34.7 us (16%)
  blocking collectives  15.2 us (7%)
  between operations  14.2 us (7%)
  local copies, waits for them, and re-layouts  9.71 us (4%)
  matrix products  8.5 us (4%)
  other arithmetic  6.55 us (3%)
  Pallas kernels  3.07 us (1%)
    all_to_all x1, waiting for transfers between devices, body(): lax.all_to_all(layer_input, 'fsdp', split_axis=1, concat_axis=0, tiled=True)  54.8 us
    all_to_all x1, waiting for transfers between devices, body(): lax.all_to_all(hat_grad, 'fsdp', split_axis=0, concat_axis=1, tiled=True)  45.8 us
    all_to_all x1, waiting for transfers between devices, body(): lax.all_to_all(grad_w, 'dp', split_axis=0, concat_axis=0, tiled=True)  16.6 us
    all_to_all x1, blocking collectives, body(): parts = lax.all_to_all(sent, 'dp', split_axis=0, concat_axis=0, tiled=True)  15.2 us
    all_to_all x1, starting transfers between devices, body(): lax.all_to_all(layer_input, 'fsdp', split_axis=1, concat_axis=0, tiled=True)  12 us
    all_to_all x1, starting transfers between devices, body(): lax.all_to_all(grad_w, 'dp', split_axis=0, concat_axis=0, tiled=True)  9.45 us
    all_to_all x1, starting transfers between devices, body(): lax.all_to_all(sent, 'fsdp', split_axis=0, concat_axis=0, tiled=True)  8.86 us
    unnamed x11, local copies, waits for them, and re-layouts  5.31 us
  transfers between devices with their start and end apart: 5, of which 5 were waited for; matrix products, arithmetic and copies ran while one was open for 5% of the time, Pallas kernels for 1%

profile of v1, /device:TPU:1, one launch (start us, length us, event | category | flops | bytes accessed | tf_op | source)
XLA Modules:
  0.0 217.8 jit_solution(14420091742901773283)
XLA Ops:
  7.2 4.1 %copy.14 = bf16[128,8192]{0,1:T(8,128)(2,1)} copy(bf16[128,8192]{1,0:T(8,128)(2,1)} %param.4) | data formatting | bytes 4194304 | tf_op args[0]
  11.2 0.0 copy-start
  11.2 12.0 %all-to-all-start.1 = ((bf16[128,16,512]{0,2,1:T(8,128)(2,1)}), bf16[128,16,512]{0,2,1:T(8,128)(2,1)}, u32[]{:S(2)}, u32[]{:S(2)}) async-start(bf16[128,16,512]{0,2,1:T(8,128)(2,1)} %bitcast.24), calls=%async_computation.1 | async-start | bytes 4194304 | tf_op jit(solution)/shard_map/all_to_all | solution.py:131
  23.2 0.0 copy-start.2
  23.2 0.0 copy-start.1
  23.2 0.0 copy-start.3
  23.2 0.0 all-gather.2.cloned.1.call-start
  23.3 0.0 copy-done
  23.3 0.5 fusion
  23.8 0.3 copy-done.2
  24.1 0.7 multiply_convert_fusion.2
  24.8 0.0 all-gather.2.cloned.1.call-update
  24.9 0.0 copy-done.1
  24.9 0.2 copy.16
  25.1 0.0 copy-done.3
  25.1 54.8 %all-to-all-done.1 = bf16[128,16,512]{0,2,1:T(8,128)(2,1)} async-done(((bf16[128,16,512]{0,2,1:T(8,128)(2,1)}), bf16[128,16,512]{0,2,1:T(8,128)(2,1)}, u32[]{:S(2)}, u32[]{:S(2)}) %all-to-all-start.1) | async-done | bytes 2097184 | tf_op jit(solution)/shard_map/all_to_all | solution.py:131
  79.9 3.9 %copy.15 = bf16[16,128,512]{2,1,0:T(8,128)(2,1)} copy(bf16[16,128,512]{1,2,0:T(8,128)(2,1)} %bitcast.3) | data formatting | bytes 4194304 | tf_op jit(solution)/shard_map/all_to_all | solution.py:131
  83.9 3.8 %all-gather.2.cloned.1.call-done = bf16[2048,512]{1,0:T(8,128)(2,1)} async-done(((bf16[128,512]{1,0:T(8,128)(2,1)}), bf16[2048,512]{1,0:T(8,128)(2,1)}) %all-gather.2.cloned.1.call-update) | async-done | bytes 2097168 | tf_op jit(solution)/shard_map/all_gather | solution.py:135
  87.7 4.3 %fusion.4 = (f32[512]{0:T(512)S(1)}, bf16[512,512]{1,0:T(8,128)(2,1)}) fusion(bf16[512,512]{0,1:T(8,128)(2,1)S(1)} %copy.16, f32[512]{0:T(512)S(1)} %broadcast_multiply_fusion, bf16[2048,512]{1,0:T(8,128)(2,1)} %all-gather.2.cloned.1.call-done, bf16[2048,512]{1,0:T(8,128)(2,1)} %bitcast.26), kind=kOutput, calls=%fused_computation.10 | convolution fusion | flops 1075052032 | bytes 5246976 | tf_op jit(solution)/shard_map/dot_general | solution.py:137
  92.0 9.5 %all-to-all-start.2 = ((bf16[32,16,512]{2,1,0:T(8,128)(2,1)}), bf16[32,16,512]{2,1,0:T(8,128)(2,1)S(1)}, u32[]{:S(2)}, u32[]{:S(2)}) async-start(bf16[32,16,512]{2,1,0:T(8,128)(2,1)} %bitcast.27), calls=%async_computation.2 | async-start | bytes 1048576 | tf_op jit(solution)/shard_map/all_to_all | solution.py:147
  101.4 16.6 %all-to-all-done.2 = bf16[32,16,512]{2,1,0:T(8,128)(2,1)S(1)} async-done(((bf16[32,16,512]{2,1,0:T(8,128)(2,1)}), bf16[32,16,512]{2,1,0:T(8,128)(2,1)S(1)}, u32[]{:S(2)}, u32[]{:S(2)}) %all-to-all-start.2) | async-done | bytes 524320 | tf_op jit(solution)/shard_map/all_to_all | solution.py:147
  118.0 0.8 shard_map.67
  118.8 15.2 %all_to_all.53.parts_ref = f32[32,16,128]{2,1,0:T(8,128)S(1)} all-to-all(f32[32,16,128]{2,1,0:T(8,128)S(1)} %shard_map.67), channel_id=1, replica_groups=mesh['dp'=32,'fsdp'=16] {'dp'}, dimensions={0} | all-to-all | bytes 524288 | tf_op jit(solution)/shard_map/all_to_all | solution.py:156
  134.0 0.9 shard_map.68
  134.9 8.9 %all-to-all-start.4 = ((f32[16,16,128]{2,1,0:T(8,128)}), f32[16,16,128]{2,1,0:T(8,128)S(1)}, u32[]{:S(2)}, u32[]{:S(2)}) async-start(f32[16,16,128]{2,1,0:T(8,128)} %shard_map.68), calls=%async_computation.4 | async-start | bytes 262144 | tf_op jit(solution)/shard_map/all_to_all | solution.py:160
  143.8 4.2 %multiply_convert_fusion = bf16[2048,512]{1,0:T(8,128)(2,1)} fusion(bf16[2048,512]{1,0:T(8,128)(2,1)} %all-gather.2.cloned.1.call-done, bf16[512,512]{1,0:T(8,128)(2,1)S(1)} %copy-done.1, f32[512]{0:T(512)S(1)} %copy-done.3), kind=kOutput, calls=%fused_computation.8 | convolution fusion | flops 1075838976 | bytes 4720640 | tf_op jit(solution)/shard_map/dot_general | solution.py:143
  148.0 5.0 %all-to-all-done.4.packed_ref = f32[16,16,128]{2,1,0:T(8,128)S(1)} async-done(((f32[16,16,128]{2,1,0:T(8,128)}), f32[16,16,128]{2,1,0:T(8,128)S(1)}, u32[]{:S(2)}, u32[]{:S(2)}) %all-to-all-start.4) | async-done | bytes 131104 | tf_op jit(solution)/shard_map/all_to_all | solution.py:160
  152.9 4.3 %all-to-all-start = ((bf16[16,128,512]{2,1,0:T(8,128)(2,1)}), bf16[16,128,512]{2,1,0:T(8,128)(2,1)}, u32[]{:S(2)}, u32[]{:S(2)}) async-start(bf16[16,128,512]{2,1,0:T(8,128)(2,1)} %bitcast.25), calls=%async_computation | async-start | bytes 4194304 | tf_op jit(solution)/shard_map/all_to_all | solution.py:148
  157.3 1.4 shard_map.69
  158.6 0.7 copy.17
  159.3 0.6 reduce
  159.9 45.8 %all-to-all-done = bf16[16,128,512]{2,1,0:T(8,128)(2,1)} async-done(((bf16[16,128,512]{2,1,0:T(8,128)(2,1)}), bf16[16,128,512]{2,1,0:T(8,128)(2,1)}, u32[]{:S(2)}, u32[]{:S(2)}) %all-to-all-start) | async-done | bytes 2097184 | tf_op jit(solution)/shard_map/all_to_all | solution.py:148
  205.7 2.1 convert_bitcast_fusion
  207.9 0.5 copy.18
  208.4 0.6 fusion.1
  209.0 2.0 fusion.3
  (4 shorter events, 0.0 us)
Async XLA Ops:
  11.2 12.0 %copy-start = (bf16[128,8192]{1,0:T(8,128)(2,1)S(1)}, bf16[128,8192]{1,0:T(8,128)(2,1)}, u32[]{:S(2)}) copy-start(bf16[128,8192]{1,0:T(8,128)(2,1)} %param.4) | copy-start | bytes 6291460
  11.2 68.7 %all-to-all-start.1 = ((bf16[128,16,512]{0,2,1:T(8,128)(2,1)}), bf16[128,16,512]{0,2,1:T(8,128)(2,1)}, u32[]{:S(2)}, u32[]{:S(2)}) async-start(bf16[128,16,512]{0,2,1:T(8,128)(2,1)} %bitcast.24), calls=%async_computation.1 | async-start | bytes 4194304 | tf_op jit(solution)/shard_map/all_to_all | solution.py:131
  23.2 0.9 copy-start.2
  23.2 1.6 copy-start.1
  23.2 1.9 copy-start.3
  23.2 64.4 %all-gather.2.cloned.1.call-start = ((), (), s32[]{:S(2)}) async-start(), calls=%async_computation.5 | async-start | bytes 2228224 | tf_op jit(solution)/shard_map/all_gather | solution.py:135
  92.0 26.1 %all-to-all-start.2 = ((bf16[32,16,512]{2,1,0:T(8,128)(2,1)}), bf16[32,16,512]{2,1,0:T(8,128)(2,1)S(1)}, u32[]{:S(2)}, u32[]{:S(2)}) async-start(bf16[32,16,512]{2,1,0:T(8,128)(2,1)} %bitcast.27), calls=%async_computation.2 | async-start | bytes 1048576 | tf_op jit(solution)/shard_map/all_to_all | solution.py:147
  134.9 18.0 %all-to-all-start.4 = ((f32[16,16,128]{2,1,0:T(8,128)}), f32[16,16,128]{2,1,0:T(8,128)S(1)}, u32[]{:S(2)}, u32[]{:S(2)}) async-start(f32[16,16,128]{2,1,0:T(8,128)} %shard_map.68), calls=%async_computation.4 | async-start | bytes 262144 | tf_op jit(solution)/shard_map/all_to_all | solution.py:160
  152.9 52.8 %all-to-all-start = ((bf16[16,128,512]{2,1,0:T(8,128)(2,1)}), bf16[16,128,512]{2,1,0:T(8,128)(2,1)}, u32[]{:S(2)}, u32[]{:S(2)}) async-start(bf16[16,128,512]{2,1,0:T(8,128)(2,1)} %bitcast.25), calls=%async_computation | async-start | bytes 4194304 | tf_op jit(solution)/shard_map/all_to_all | solution.py:148
Sparse Core Ops, SparseCore 0:
  26.2 61.4 all-gather.1

commit v2 on v1

--- a/solution.py
+++ b/solution.py
@@ -11,6 +11,7 @@
 EPS_SUM = 1e-06
 REPLICAS = 32
 LANES = 128
+PARAMS = pltpu.CompilerParams(vmem_limit_bytes=32 * 1024 * 1024)
 
 
 def pack_gram(gram):
@@ -109,7 +110,7 @@
     for replica in range(REPLICAS):
         shard = shards_ref[replica * width : (replica + 1) * width, :].astype(jnp.float32)
         total += weights_w[replica : replica + 1, :] * shard
-    weight_ref[...] = total.T.astype(jnp.bfloat16)
+    weight_ref[...] = total.astype(jnp.bfloat16)
     for part in range(4):
         piece = parts_ref[:, 8 + part, :]
         gain_ref[:, part * LANES : (part + 1) * LANES] = jnp.sum(
@@ -121,18 +122,75 @@
     return pl.pallas_call(
         kernel,
         out_shape=out_shape,
-        compiler_params=pltpu.CompilerParams(vmem_limit_bytes=32 * 1024 * 1024),
+        compiler_params=PARAMS,
     )(*args)
+
+
+def norm_kernel(input_ref, blocks_ref):
+    input32 = input_ref[...].astype(jnp.float32)
+    square = jnp.mean(input32 * input32, axis=1, keepdims=True)
+    normed = (input32 * lax.rsqrt(square + EPS_NORM)).astype(jnp.bfloat16)
+    width = blocks_ref.shape[2]
+    for owner in range(blocks_ref.shape[0]):
+        blocks_ref[owner, :, :] = normed[:, owner * width : (owner + 1) * width]
+
+
+def input_kernel(input_ref, cotangent_ref, weight_ref, out_ref, hat_ref, total_ref):
+    step, steps = pl.program_id(0), pl.num_programs(0)
+    width = weight_ref.shape[0]
+
+    @pl.when(step == 0)
+    def _():
+        total_ref[...] = jnp.zeros_like(total_ref)
+
+    hat = lax.dot_general(
+        cotangent_ref[...],
+        weight_ref[...],
+        (((1,), (1,)), ((), ())),
+        preferred_element_type=jnp.float32,
+    ).astype(jnp.bfloat16)
+    columns = pl.ds(pl.multiple_of(step * width, width), width)
+    hat_ref[:, columns] = hat
+    total_ref[...] += hat.astype(jnp.float32) * input_ref[:, columns].astype(jnp.float32)
+
+    @pl.when(step == steps - 1)
+    def _():
+        model = input_ref.shape[1]
+        square = jnp.zeros_like(total_ref)
+        for part in range(model // width):
+            piece = input_ref[:, part * width : (part + 1) * width].astype(jnp.float32)
+            square += piece * piece
+        inverse_rms = lax.rsqrt(jnp.sum(square, axis=1, keepdims=True) / model + EPS_NORM)
+        mean_term = jnp.sum(total_ref[...], axis=1, keepdims=True) / model * inverse_rms
+        factor = inverse_rms * mean_term
+        for part in range(model // width):
+            at = slice(part * width, (part + 1) * width)
+            piece = input_ref[:, at].astype(jnp.float32)
+            out_ref[:, at] = (
+                inverse_rms * (hat_ref[:, at].astype(jnp.float32) - piece * factor)
+            ).astype(jnp.bfloat16)
 
 
 def body(layer_input, norm_gain, value_weight, value_cotangent):
     tokens, model = layer_input.shape
-    peers = lax.axis_size("fsdp")
-    columns = lax.all_to_all(layer_input, "fsdp", split_axis=1, concat_axis=0, tiled=True)
-    input32 = layer_input.astype(jnp.float32)
-    inverse_rms = lax.rsqrt(jnp.mean(input32 * input32, axis=1, keepdims=True) + EPS_NORM)
-    scaled_cotangent = (value_cotangent.astype(jnp.float32) * inverse_rms).astype(jnp.bfloat16)
-    cotangent = lax.all_gather(scaled_cotangent, "fsdp", axis=0, tiled=True)
+    peers, width = lax.axis_size("fsdp"), value_cotangent.shape[1]
+    own = model // peers
+    cotangent = lax.all_gather(value_cotangent, "fsdp", axis=0, tiled=True)
+    step = 16
+    blocks = pl.pallas_call(
+        norm_kernel,
+        grid=(tokens // step,),
+        in_specs=[pl.BlockSpec((step, model), lambda i: (i, 0))],
+        out_specs=pl.BlockSpec((peers, step, own), lambda i: (0, i, 0)),
+        out_shape=jax.ShapeDtypeStruct((peers, tokens, own), jnp.bfloat16),
+        compiler_params=PARAMS,
+    )(layer_input)
+    columns = lax.all_to_all(blocks, "fsdp", split_axis=0, concat_axis=0, tiled=True)
+    columns = columns.reshape(peers * tokens, own)
+    scaled_weight = (value_weight.astype(jnp.float32) * norm_gain[:, None]).astype(jnp.bfloat16)
+    scaled_weight, cotangent = lax.optimization_barrier((scaled_weight, cotangent))
+    all_weight = lax.all_gather(scaled_weight, "fsdp", axis=0, tiled=True)
+
     grad_scale = 1.0 / math.sqrt(cotangent.shape[0])
     grad = lax.dot_general(
         cotangent, columns, (((0,), (0,)), ((), ())), preferred_element_type=jnp.float32
@@ -140,12 +198,7 @@
     grad_w = (grad * (norm_gain * grad_scale)[None, :]).astype(jnp.bfloat16)
     weight_t = value_weight.T.astype(jnp.float32)
     grad_g = (jnp.sum(grad * weight_t, axis=0, keepdims=True) * grad_scale).astype(jnp.bfloat16)
-    back = lax.dot_general(
-        cotangent, value_weight, (((1,), (1,)), ((), ())), preferred_element_type=jnp.float32
-    )
-    hat_grad = (back * norm_gain[None, :]).astype(jnp.bfloat16)
     shards = lax.all_to_all(grad_w, "dp", split_axis=0, concat_axis=0, tiled=True)
-    returned = lax.all_to_all(hat_grad, "fsdp", split_axis=0, concat_axis=1, tiled=True)
 
     sent = kernel_call(
         gram_kernel,
@@ -161,17 +214,33 @@
     weight_update, gain_update = kernel_call(
         combine_kernel,
         (
-            jax.ShapeDtypeStruct((shards.shape[1], shards.shape[0] // REPLICAS), jnp.bfloat16),
-            jax.ShapeDtypeStruct((1, shards.shape[1]), jnp.bfloat16),
+            jax.ShapeDtypeStruct((shards.shape[0] // REPLICAS, own), jnp.bfloat16),
+            jax.ShapeDtypeStruct((1, own), jnp.bfloat16),
         ),
         packed,
         shards,
         parts,
     )
-    hat32 = returned.astype(jnp.float32)
-    mean_term = jnp.mean(hat32 * input32, axis=1, keepdims=True)
-    input_grad = (hat32 - input32 * (inverse_rms * inverse_rms * mean_term)).astype(jnp.bfloat16)
-    return (input_grad, weight_update, gain_update[0])
+    input_grad = pl.pallas_call(
+        input_kernel,
+        grid=(peers,),
+        in_specs=[
+            pl.BlockSpec((tokens, model), lambda i: (0, 0)),
+            pl.BlockSpec((tokens, width), lambda i: (0, 0)),
+            pl.BlockSpec((own, width), lambda i: (i, 0)),
+        ],
+        out_specs=pl.BlockSpec((tokens, model), lambda i: (0, 0)),
+        out_shape=jax.ShapeDtypeStruct((tokens, model), jnp.bfloat16),
+        scratch_shapes=[
+            pltpu.VMEM((tokens, model), jnp.bfloat16),
+            pltpu.VMEM((tokens, own), jnp.float32),
+        ],
+        compiler_params=PARAMS,
+        cost_estimate=pl.CostEstimate(
+            flops=2 * tokens * model * width, bytes_accessed=2 * model * (width + 2 * tokens), transcendentals=0
+        ),
+    )(layer_input, value_cotangent, all_weight)
+    return (input_grad, weight_update.T, gain_update[0])
 
 
 def solution(mesh):

time: 218 us -> 224 us (1.028)
  starting transfers between devices: 34.7 us -> 14 us
  blocking collectives: 15.2 us -> 32.5 us
  Pallas kernels: 3.07 us -> 14.7 us
  waiting for transfers between devices: 126 us -> 133 us
  matrix products: 8.5 us -> 4.03 us
  other arithmetic: 6.55 us -> 4.16 us
    all_gather x1 -> x2, waiting for transfers between devices: 3.79 us -> 49.3 us  [the longest x1 49.3 us: body(): cotangent = lax.all_gather(value_cotangent, 'fsdp', axis=0, tiled=True)]
    all_to_all x3 -> x1, waiting for transfers between devices: 106 us -> 69.9 us  [body(): lax.all_to_all(blocks, 'fsdp', split_axis=0, concat_axis=0, tiled=True)]
    all_to_all x3 -> x1, starting transfers between devices: 25.2 us -> 4.55 us  [body(): lax.all_to_all(blocks, 'fsdp', split_axis=0, concat_axis=0, tiled=True)]
    all_to_all x0 -> x1, blocking collectives: none -> 15.9 us  [body(): lax.all_to_all(sent, 'fsdp', split_axis=0, concat_axis=0, tiled=True)]
    pallas_call x3 -> x5, Pallas kernels: 3.07 us -> 14.7 us  [the longest x1 8.26 us: body(): pl.pallas_call(input_kernel, grid=(peers,), in_specs=[pl.BlockSpec((token...]
    dot_general x1 -> x0, matrix products: 4.2 us -> none  [body(): lax.dot_general(cotangent, value_weight, (((1,), (1,)), ((), ())), prefer...]
    all_to_all x1 -> x0, local copies, waits for them, and re-layouts: 3.93 us -> none  [body(): lax.all_to_all(layer_input, 'fsdp', split_axis=1, concat_axis=0, tiled=True)]
    all_to_all x1, waiting for transfers between devices: 16.6 us -> 12.8 us  [body(): lax.all_to_all(grad_w, 'dp', split_axis=0, concat_axis=0, tiled=True)]
  transfers between devices with their start and end apart: 5 -> 4, of which waited for: 5 -> 3; matrix products, arithmetic and copies ran while one was open for 5% -> 5% of each run, Pallas kernels for 1% -> 3%
where the time goes in v2:
time: 224 us
  waiting for transfers between devices  133 us (59%)
  blocking collectives  32.5 us (15%)
  Pallas kernels  14.7 us (7%)
  between operations  14.1 us (6%)
  starting transfers between devices  14 us (6%)
  local copies, waits for them, and re-layouts  7.62 us (3%)
  other arithmetic  4.16 us (2%)
  matrix products  4.03 us (2%)
    all_to_all x1, waiting for transfers between devices, body(): lax.all_to_all(blocks, 'fsdp', split_axis=0, concat_axis=0, tiled=True)  69.9 us
    all_gather x1, waiting for transfers between devices, body(): cotangent = lax.all_gather(value_cotangent, 'fsdp', axis=0, tiled=True)  49.3 us
    all_to_all x1, blocking collectives, body(): parts = lax.all_to_all(sent, 'dp', split_axis=0, concat_axis=0, tiled=True)  16.6 us
    all_to_all x1, blocking collectives, body(): lax.all_to_all(sent, 'fsdp', split_axis=0, concat_axis=0, tiled=True)  15.9 us
    all_to_all x1, waiting for transfers between devices, body(): lax.all_to_all(grad_w, 'dp', split_axis=0, concat_axis=0, tiled=True)  12.8 us
    all_to_all x1, starting transfers between devices, body(): lax.all_to_all(grad_w, 'dp', split_axis=0, concat_axis=0, tiled=True)  9.39 us
    pallas_call x1, Pallas kernels, body(): pl.pallas_call(input_kernel, grid=(peers,), in_specs=[pl.BlockSpec((token...  8.26 us
    unnamed x12, local copies, waits for them, and re-layouts  4.98 us
  transfers between devices with their start and end apart: 4, of which 3 were waited for; matrix products, arithmetic and copies ran while one was open for 5% of the time, Pallas kernels for 3%

profile of v2, /device:TPU:1, one launch (start us, length us, event | category | flops | bytes accessed | tf_op | source)
XLA Modules:
  0.0 223.8 jit_solution(3038701905603833641)
XLA Ops:
  7.2 0.0 all-gather.3.cloned.1.call-start
  7.2 0.7 all-gather.3.cloned.1.call-update
  7.9 0.0 all-gather.5.cloned.1.call-start
  7.9 2.0 fusion
  10.0 49.3 %all-gather.3.cloned.1.call-done = bf16[2048,512]{1,0:T(8,128)(2,1)} async-done(((bf16[128,512]{1,0:T(8,128)(2,1)}), bf16[2048,512]{1,0:T(8,128)(2,1)}) %all-gather.3.cloned.1.call-update) | async-done | bytes 2097168 | tf_op jit(solution)/shard_map/all_gather | solution.py:178
  59.2 0.0 all-gather.5.cloned.1.call-update
  59.3 0.0 copy-start
  59.3 1.6 copy-done
  60.9 3.8 %shard_map.68 = bf16[16,128,512]{2,1,0:T(8,128)(2,1)} custom-call(bf16[128,8192]{1,0:T(8,128)(2,1)S(1)} %copy-done), custom_call_target="tpu_custom_call" | custom-call | tf_op jit(solution)/shard_map/pallas_call | solution.py:180
  64.6 0.0 copy-start.5
  64.6 4.6 %all-to-all-start = ((bf16[16,128,512]{2,1,0:T(8,128)(2,1)}), bf16[16,128,512]{2,1,0:T(8,128)(2,1)S(1)}, u32[]{:S(2)}, u32[]{:S(2)}) async-start(bf16[16,128,512]{2,1,0:T(8,128)(2,1)} %shard_map.68), calls=%async_computation | async-start | bytes 4194304 | tf_op jit(solution)/shard_map/all_to_all | solution.py:188
  69.2 0.0 copy-done.5
  69.2 69.9 %all-to-all-done = bf16[16,128,512]{2,1,0:T(8,128)(2,1)S(1)} async-done(((bf16[16,128,512]{2,1,0:T(8,128)(2,1)}), bf16[16,128,512]{2,1,0:T(8,128)(2,1)S(1)}, u32[]{:S(2)}, u32[]{:S(2)}) %all-to-all-start) | async-done | bytes 2097184 | tf_op jit(solution)/shard_map/all_to_all | solution.py:188
  139.1 4.0 %multiply_convert_fusion = (bf16[512,512]{1,0:T(8,128)(2,1)}, f32[512,512]{1,0:T(8,128)}) fusion(f32[512]{0:T(512)S(1)} %broadcast_multiply_fusion, bf16[2048,512]{1,0:T(8,128)(2,1)} %all-gather.3.cloned.1.call-done, bf16[2048,512]{1,0:T(8,128)(2,1)S(1)} %bitcast.16), kind=kOutput, calls=%fused_computation.5 | convolution fusion | flops 1074266112 | bytes 5769216 | tf_op jit(solution)/shard_map/dot_general | solution.py:195
  143.1 0.0 copy-start.4
  143.1 9.4 %all-to-all-start.1 = ((bf16[32,16,512]{2,1,0:T(8,128)(2,1)}), bf16[32,16,512]{2,1,0:T(8,128)(2,1)S(1)}, u32[]{:S(2)}, u32[]{:S(2)}) async-start(bf16[32,16,512]{2,1,0:T(8,128)(2,1)} %bitcast.17), calls=%async_computation.1 | async-start | bytes 1048576 | tf_op jit(solution)/shard_map/all_to_all | solution.py:201
  152.5 2.6 %copy.7 = f32[512,512]{0,1:T(8,128)} copy(f32[512,512]{1,0:T(8,128)} %get-tuple-element.12) | data formatting | bytes 2097152 | tf_op jit(solution)/shard_map/dot_general | solution.py:195
  155.1 0.0 copy-done.4
  155.1 0.0 copy-start.1
  155.1 0.0 copy-start.3
  155.1 1.6 fusion.2
  156.7 12.8 %all-to-all-done.1 = bf16[32,16,512]{2,1,0:T(8,128)(2,1)S(1)} async-done(((bf16[32,16,512]{2,1,0:T(8,128)(2,1)}), bf16[32,16,512]{2,1,0:T(8,128)(2,1)S(1)}, u32[]{:S(2)}, u32[]{:S(2)}) %all-to-all-start.1) | async-done | bytes 524320 | tf_op jit(solution)/shard_map/all_to_all | solution.py:201
  169.5 0.8 shard_map.69
  170.3 16.6 %all_to_all.26.parts_ref = f32[32,16,128]{2,1,0:T(8,128)S(1)} all-to-all(f32[32,16,128]{2,1,0:T(8,128)S(1)} %shard_map.69), channel_id=1, replica_groups=mesh['dp'=32,'fsdp'=16] {'dp'}, dimensions={0} | all-to-all | bytes 524288 | tf_op jit(solution)/shard_map/all_to_all | solution.py:209
  186.9 0.3 shard_map.70
  187.2 15.9 %all_to_all.27.packed_ref = f32[16,16,128]{2,1,0:T(8,128)S(1)} all-to-all(f32[16,16,128]{2,1,0:T(8,128)S(1)} %shard_map.70), channel_id=1, replica_groups=mesh['dp'=32,'fsdp'=16] {'fsdp'}, dimensions={0} | all-to-all | bytes 262144 | tf_op jit(solution)/shard_map/all_to_all | solution.py:213
  203.1 1.6 shard_map.71
  204.7 0.6 reduce
  205.3 0.0 all-gather.5.cloned.1.call-done.weight_ref
  205.3 0.0 copy-done.1
  205.3 0.0 copy-done.3
  205.3 0.0 copy-start.2
  205.3 3.4 %copy-done.2 = bf16[8192,512]{1,0:T(8,128)(2,1)S(1)} copy-done((bf16[8192,512]{1,0:T(8,128)(2,1)S(1)}, bf16[8192,512]{1,0:T(8,128)(2,1)}, u32[]{:S(2)}) %copy-start.2) | copy-done | bytes 8388632
  208.7 8.3 %shard_map.67 = bf16[128,8192]{1,0:T(8,128)(2,1)} custom-call(bf16[128,8192]{1,0:T(8,128)(2,1)S(1)} %copy-done.1, bf16[128,512]{1,0:T(8,128)(2,1)S(1)} %copy-done.3, bf16[8192,512]{1,0:T(8,128)(2,1)S(1)} %copy-done.2), custom_call_target="tpu_custom_call" | custom-call | flops 1073741824 | bytes 12582912 | tf_op jit(solution)/shard_map/pallas_call | solution.py:224
  (2 shorter events, 0.0 us)
Async XLA Ops:
  7.2 52.1 %all-gather.3.cloned.1.call-start = ((), (), s32[]{:S(2)}) async-start(), calls=%async_computation.4 | async-start | bytes 2228224 | tf_op jit(solution)/shard_map/all_gather | solution.py:178
  7.9 197.4 %all-gather.5.cloned.1.call-start = ((), (), s32[]{:S(2)}) async-start(), calls=%async_computation.5 | async-start | bytes 8912896 | tf_op jit(solution)/shard_map/all_gather | solution.py:192
  59.3 1.6 copy-start
  64.6 4.6 %copy-start.5 = (f32[512]{0:T(512)S(1)}, f32[512]{0:T(512)}, u32[]{:S(2)}) copy-start(f32[512]{0:T(512)} %param.5) | copy-start | bytes 6148
  64.6 74.4 %all-to-all-start = ((bf16[16,128,512]{2,1,0:T(8,128)(2,1)}), bf16[16,128,512]{2,1,0:T(8,128)(2,1)S(1)}, u32[]{:S(2)}, u32[]{:S(2)}) async-start(bf16[16,128,512]{2,1,0:T(8,128)(2,1)} %shard_map.68), calls=%async_computation | async-start | bytes 4194304 | tf_op jit(solution)/shard_map/all_to_all | solution.py:188
  143.1 12.0 %copy-start.4 = (bf16[512,512]{1,0:T(8,128)(2,1)S(1)}, bf16[512,512]{1,0:T(8,128)(2,1)}, u32[]{:S(2)}) copy-start(bf16[512,512]{1,0:T(8,128)(2,1)} %param.6) | copy-start | bytes 1572868
  143.1 26.4 %all-to-all-start.1 = ((bf16[32,16,512]{2,1,0:T(8,128)(2,1)}), bf16[32,16,512]{2,1,0:T(8,128)(2,1)S(1)}, u32[]{:S(2)}, u32[]{:S(2)}) async-start(bf16[32,16,512]{2,1,0:T(8,128)(2,1)} %bitcast.17), calls=%async_computation.1 | async-start | bytes 1048576 | tf_op jit(solution)/shard_map/all_to_all | solution.py:201
  155.1 50.1 %copy-start.1 = (bf16[128,8192]{1,0:T(8,128)(2,1)S(1)}, bf16[128,8192]{1,0:T(8,128)(2,1)}, u32[]{:S(2)}) copy-start(bf16[128,8192]{1,0:T(8,128)(2,1)} %input_ref.3) | copy-start | bytes 6291460
  155.1 50.1 %copy-start.3 = (bf16[128,512]{1,0:T(8,128)(2,1)S(1)}, bf16[128,512]{1,0:T(8,128)(2,1)}, u32[]{:S(2)}) copy-start(bf16[128,512]{1,0:T(8,128)(2,1)} %cotangent_ref.1) | copy-start | bytes 393220
  205.3 3.4 %copy-start.2 = (bf16[8192,512]{1,0:T(8,128)(2,1)S(1)}, bf16[8192,512]{1,0:T(8,128)(2,1)}, u32[]{:S(2)}) copy-start(bf16[8192,512]{1,0:T(8,128)(2,1)} %all-gather.5.cloned.1.call-done.weight_ref) | copy-start | bytes 25165828
Sparse Core Ops, SparseCore 0:
  10.1 49.0 all-gather.2
  61.4 97.9 all-gather.4

commit v3 on v2

--- a/solution.py
+++ b/solution.py
@@ -12,6 +12,7 @@
 REPLICAS = 32
 LANES = 128
 PARAMS = pltpu.CompilerParams(vmem_limit_bytes=32 * 1024 * 1024)
+LARGE = pltpu.CompilerParams(vmem_limit_bytes=60 * 1024 * 1024)
 
 
 def pack_gram(gram):
@@ -126,43 +127,39 @@
     )(*args)
 
 
-def norm_kernel(input_ref, blocks_ref):
+def norm_kernel(input_ref, blocks_ref, scale_ref):
     input32 = input_ref[...].astype(jnp.float32)
     square = jnp.mean(input32 * input32, axis=1, keepdims=True)
-    normed = (input32 * lax.rsqrt(square + EPS_NORM)).astype(jnp.bfloat16)
+    inverse_rms = lax.rsqrt(square + EPS_NORM)
+    scale_ref[...] = jnp.broadcast_to(inverse_rms, scale_ref.shape)
+    normed = (input32 * inverse_rms).astype(jnp.bfloat16)
     width = blocks_ref.shape[2]
     for owner in range(blocks_ref.shape[0]):
         blocks_ref[owner, :, :] = normed[:, owner * width : (owner + 1) * width]
 
 
-def input_kernel(input_ref, cotangent_ref, weight_ref, out_ref, hat_ref, total_ref):
+def input_kernel(input_ref, cotangent_ref, weight_ref, scale_ref, out_ref, hat_ref, total_ref):
     step, steps = pl.program_id(0), pl.num_programs(0)
-    width = weight_ref.shape[0]
+    model, width = input_ref.shape[1], weight_ref.shape[2]
 
     @pl.when(step == 0)
     def _():
         total_ref[...] = jnp.zeros_like(total_ref)
 
-    hat = lax.dot_general(
-        cotangent_ref[...],
-        weight_ref[...],
-        (((1,), (1,)), ((), ())),
-        preferred_element_type=jnp.float32,
-    ).astype(jnp.bfloat16)
-    columns = pl.ds(pl.multiple_of(step * width, width), width)
-    hat_ref[:, columns] = hat
-    total_ref[...] += hat.astype(jnp.float32) * input_ref[:, columns].astype(jnp.float32)
+    for block in range(weight_ref.shape[0]):
+        hat = jnp.dot(
+            cotangent_ref[...], weight_ref[block], preferred_element_type=jnp.float32
+        ).astype(jnp.bfloat16)
+        at = (step * weight_ref.shape[0] + block) * width
+        columns = pl.ds(pl.multiple_of(at, width), width)
+        hat_ref[:, columns] = hat
+        total_ref[...] += hat.astype(jnp.float32) * input_ref[:, columns].astype(jnp.float32)
 
     @pl.when(step == steps - 1)
     def _():
-        model = input_ref.shape[1]
-        square = jnp.zeros_like(total_ref)
-        for part in range(model // width):
-            piece = input_ref[:, part * width : (part + 1) * width].astype(jnp.float32)
-            square += piece * piece
-        inverse_rms = lax.rsqrt(jnp.sum(square, axis=1, keepdims=True) / model + EPS_NORM)
-        mean_term = jnp.sum(total_ref[...], axis=1, keepdims=True) / model * inverse_rms
-        factor = inverse_rms * mean_term
+        inverse_rms = scale_ref[:, 0:1]
+        factor = jnp.sum(total_ref[...], axis=1, keepdims=True) / model
+        factor = inverse_rms * inverse_rms * factor
         for part in range(model // width):
             at = slice(part * width, (part + 1) * width)
             piece = input_ref[:, at].astype(jnp.float32)
@@ -176,27 +173,33 @@
     peers, width = lax.axis_size("fsdp"), value_cotangent.shape[1]
     own = model // peers
     cotangent = lax.all_gather(value_cotangent, "fsdp", axis=0, tiled=True)
-    step = 16
-    blocks = pl.pallas_call(
+    step = 32
+    blocks, scale = pl.pallas_call(
         norm_kernel,
         grid=(tokens // step,),
         in_specs=[pl.BlockSpec((step, model), lambda i: (i, 0))],
-        out_specs=pl.BlockSpec((peers, step, own), lambda i: (0, i, 0)),
-        out_shape=jax.ShapeDtypeStruct((peers, tokens, own), jnp.bfloat16),
-        compiler_params=PARAMS,
+        out_specs=(
+            pl.BlockSpec((peers, step, own), lambda i: (0, i, 0)),
+            pl.BlockSpec((step, LANES), lambda i: (i, 0)),
+        ),
+        out_shape=(
+            jax.ShapeDtypeStruct((peers, tokens, own), jnp.bfloat16),
+            jax.ShapeDtypeStruct((tokens, LANES), jnp.float32),
+        ),
+        compiler_params=LARGE,
     )(layer_input)
     columns = lax.all_to_all(blocks, "fsdp", split_axis=0, concat_axis=0, tiled=True)
     columns = columns.reshape(peers * tokens, own)
-    scaled_weight = (value_weight.astype(jnp.float32) * norm_gain[:, None]).astype(jnp.bfloat16)
-    scaled_weight, cotangent = lax.optimization_barrier((scaled_weight, cotangent))
-    all_weight = lax.all_gather(scaled_weight, "fsdp", axis=0, tiled=True)
+    weight_t = value_weight.T.astype(jnp.float32)
+    scaled_weight = (weight_t * norm_gain[None, :]).astype(jnp.bfloat16)
+    scaled_weight, columns = lax.optimization_barrier((scaled_weight, columns))
+    all_weight = lax.all_gather(scaled_weight, "fsdp", axis=0)
 
     grad_scale = 1.0 / math.sqrt(cotangent.shape[0])
     grad = lax.dot_general(
         cotangent, columns, (((0,), (0,)), ((), ())), preferred_element_type=jnp.float32
     )
     grad_w = (grad * (norm_gain * grad_scale)[None, :]).astype(jnp.bfloat16)
-    weight_t = value_weight.T.astype(jnp.float32)
     grad_g = (jnp.sum(grad * weight_t, axis=0, keepdims=True) * grad_scale).astype(jnp.bfloat16)
     shards = lax.all_to_all(grad_w, "dp", split_axis=0, concat_axis=0, tiled=True)
 
@@ -221,13 +224,15 @@
         shards,
         parts,
     )
+    group = 4
     input_grad = pl.pallas_call(
         input_kernel,
-        grid=(peers,),
+        grid=(peers // group,),
         in_specs=[
             pl.BlockSpec((tokens, model), lambda i: (0, 0)),
             pl.BlockSpec((tokens, width), lambda i: (0, 0)),
-            pl.BlockSpec((own, width), lambda i: (i, 0)),
+            pl.BlockSpec((group, width, own), lambda i: (i, 0, 0)),
+            pl.BlockSpec((tokens, LANES), lambda i: (0, 0)),
         ],
         out_specs=pl.BlockSpec((tokens, model), lambda i: (0, 0)),
         out_shape=jax.ShapeDtypeStruct((tokens, model), jnp.bfloat16),
@@ -235,11 +240,11 @@
             pltpu.VMEM((tokens, model), jnp.bfloat16),
             pltpu.VMEM((tokens, own), jnp.float32),
         ],
-        compiler_params=PARAMS,
+        compiler_params=LARGE,
         cost_estimate=pl.CostEstimate(
             flops=2 * tokens * model * width, bytes_accessed=2 * model * (width + 2 * tokens), transcendentals=0
         ),
-    )(layer_input, value_cotangent, all_weight)
+    )(layer_input, value_cotangent, all_weight, scale)
     return (input_grad, weight_update.T, gain_update[0])
 
 

time: 224 us -> 169 us (0.75)
  waiting for transfers between devices: 133 us -> 79.8 us
  starting transfers between devices: 14 us -> 21.5 us
  local copies, waits for them, and re-layouts: 7.62 us -> 0.22 us
  other arithmetic: 4.16 us -> 1.5 us
    all_gather x1, waiting for transfers between devices: 49.3 us -> 7.68 us  [body(): cotangent = lax.all_gather(value_cotangent, 'fsdp', axis=0, tiled=True)]
    all_to_all x1, waiting for transfers between devices: 69.9 us -> 54.8 us  [body(): lax.all_to_all(blocks, 'fsdp', split_axis=0, concat_axis=0, tiled=True)]
    all_to_all x1, starting transfers between devices: 4.55 us -> 12 us  [body(): lax.all_to_all(blocks, 'fsdp', split_axis=0, concat_axis=0, tiled=True)]
    unnamed x12 -> x5, local copies, waits for them, and re-layouts: 4.98 us -> 0.22 us
    all_to_all x1, waiting for transfers between devices: 12.8 us -> 16.6 us  [body(): lax.all_to_all(grad_w, 'dp', split_axis=0, concat_axis=0, tiled=True)]
    dot_general x1 -> x0, local copies, waits for them, and re-layouts: 2.64 us -> none  [body(): lax.dot_general(cotangent, columns, (((0,), (0,)), ((), ())), preferred_e...]
  transfers between devices with their start and end apart: 4 -> 4, of which waited for: 3 -> 3; matrix products, arithmetic and copies ran while one was open for 5% -> 3% of each run, Pallas kernels for 3% -> 2%
where the time goes in v3:
time: 169 us
  waiting for transfers between devices  79.8 us (47%)
  blocking collectives  33 us (20%)
  starting transfers between devices  21.5 us (13%)
  Pallas kernels  15 us (9%)
  between operations  14.1 us (8%)
  matrix products  3.71 us (2%)
    all_to_all x1, waiting for transfers between devices, body(): lax.all_to_all(blocks, 'fsdp', split_axis=0, concat_axis=0, tiled=True)  54.8 us
    all_to_all x1, blocking collectives, body(): lax.all_to_all(sent, 'fsdp', split_axis=0, concat_axis=0, tiled=True)  17.8 us
    all_to_all x1, waiting for transfers between devices, body(): lax.all_to_all(grad_w, 'dp', split_axis=0, concat_axis=0, tiled=True)  16.6 us
    all_to_all x1, blocking collectives, body(): parts = lax.all_to_all(sent, 'dp', split_axis=0, concat_axis=0, tiled=True)  15.2 us
    all_to_all x1, starting transfers between devices, body(): lax.all_to_all(blocks, 'fsdp', split_axis=0, concat_axis=0, tiled=True)  12 us
    all_to_all x1, starting transfers between devices, body(): lax.all_to_all(grad_w, 'dp', split_axis=0, concat_axis=0, tiled=True)  9.45 us
    pallas_call x1, Pallas kernels, body(): pl.pallas_call(input_kernel, grid=(peers // group,), in_specs=[pl.BlockSp...  8.13 us
    all_gather x1, waiting for transfers between devices, body(): cotangent = lax.all_gather(value_cotangent, 'fsdp', axis=0, tiled=True)  7.68 us
  transfers between devices with their start and end apart: 4, of which 3 were waited for; matrix products, arithmetic and copies ran while one was open for 3% of the time, Pallas kernels for 2%

profile of v3, /device:TPU:1, one launch (start us, length us, event | category | flops | bytes accessed | tf_op | source)
XLA Modules:
  0.0 168.8 jit_solution(18226562475475992271)
XLA Ops:
  7.2 4.2 %shard_map.67 = (bf16[16,128,512]{2,1,0:T(8,128)(2,1)}, f32[128,128]{1,0:T(8,128)}) custom-call(bf16[128,8192]{1,0:T(8,128)(2,1)} %input_ref.3), custom_call_target="tpu_custom_call" | custom-call | tf_op jit(solution)/shard_map/pallas_call | solution.py:177
  11.4 0.0 copy-start
  11.4 0.0 copy-start.1
  11.4 12.0 %all-to-all-start = ((bf16[16,128,512]{2,1,0:T(8,128)(2,1)}), bf16[16,128,512]{2,1,0:T(8,128)(2,1)S(1)}, u32[]{:S(2)}, u32[]{:S(2)}) async-start(bf16[16,128,512]{2,1,0:T(8,128)(2,1)} %get-tuple-element.9), calls=%async_computation | async-start | bytes 4194304 | tf_op jit(solution)/shard_map/all_to_all | solution.py:191
  23.3 0.0 all-gather.4.cloned.1.call-start
  23.4 0.7 all-gather.4.cloned.1.call-update
  24.1 0.0 all-gather.6.cloned.1.call-start
  24.1 0.0 copy-done
  24.1 0.2 copy.7
  24.4 0.0 copy-done.1
  24.4 0.9 fusion.2
  25.3 54.8 %all-to-all-done = bf16[16,128,512]{2,1,0:T(8,128)(2,1)S(1)} async-done(((bf16[16,128,512]{2,1,0:T(8,128)(2,1)}), bf16[16,128,512]{2,1,0:T(8,128)(2,1)S(1)}, u32[]{:S(2)}, u32[]{:S(2)}) %all-to-all-start) | async-done | bytes 2097184 | tf_op jit(solution)/shard_map/all_to_all | solution.py:191
  80.1 0.0 all-gather.6.cloned.1.call-update
  80.1 7.7 %all-gather.4.cloned.1.call-done = bf16[2048,512]{1,0:T(8,128)(2,1)} async-done(((bf16[128,512]{1,0:T(8,128)(2,1)}), bf16[2048,512]{1,0:T(8,128)(2,1)}) %all-gather.4.cloned.1.call-update) | async-done | bytes 2097168 | tf_op jit(solution)/shard_map/all_gather | solution.py:175
  87.8 3.7 %fusion.1 = (f32[512]{0:T(512)S(1)}, bf16[512,512]{0,1:T(8,128)(2,1)}) fusion(bf16[512,512]{0,1:T(8,128)(2,1)S(1)} %copy.7, f32[512]{0:T(512)S(1)} %broadcast_multiply_fusion, bf16[2048,512]{1,0:T(8,128)(2,1)S(1)} %bitcast.16, bf16[2048,512]{1,0:T(8,128)(2,1)} %all-gather.4.cloned.1.call-done), kind=kOutput, calls=%fused_computation.3 | convolution fusion | flops 1075052032 | bytes 5246976 | tf_op jit(solution)/shard_map/dot_general | solution.py:199
  91.5 9.4 %all-to-all-start.1 = ((bf16[32,16,512]{2,1,0:T(8,128)(2,1)}), bf16[32,16,512]{2,1,0:T(8,128)(2,1)S(1)}, u32[]{:S(2)}, u32[]{:S(2)}) async-start(bf16[32,16,512]{2,1,0:T(8,128)(2,1)} %bitcast.4), calls=%async_computation.1 | async-start | bytes 1048576 | tf_op jit(solution)/shard_map/all_to_all | solution.py:204
  101.0 16.6 %all-to-all-done.1 = bf16[32,16,512]{2,1,0:T(8,128)(2,1)S(1)} async-done(((bf16[32,16,512]{2,1,0:T(8,128)(2,1)}), bf16[32,16,512]{2,1,0:T(8,128)(2,1)S(1)}, u32[]{:S(2)}, u32[]{:S(2)}) %all-to-all-start.1) | async-done | bytes 524320 | tf_op jit(solution)/shard_map/all_to_all | solution.py:204
  117.6 0.8 shard_map.69
  118.4 15.2 %all_to_all.26.parts_ref = f32[32,16,128]{2,1,0:T(8,128)S(1)} all-to-all(f32[32,16,128]{2,1,0:T(8,128)S(1)} %shard_map.69), channel_id=1, replica_groups=mesh['dp'=32,'fsdp'=16] {'dp'}, dimensions={0} | all-to-all | bytes 524288 | tf_op jit(solution)/shard_map/all_to_all | solution.py:212
  133.5 0.3 shard_map.70
  133.8 17.8 %all_to_all.27.packed_ref = f32[16,16,128]{2,1,0:T(8,128)S(1)} all-to-all(f32[16,16,128]{2,1,0:T(8,128)S(1)} %shard_map.70), channel_id=1, replica_groups=mesh['dp'=32,'fsdp'=16] {'fsdp'}, dimensions={0} | all-to-all | bytes 262144 | tf_op jit(solution)/shard_map/all_to_all | solution.py:216
  151.6 1.6 shard_map.71
  153.3 0.6 reduce.1
  153.8 0.0 all-gather.6.cloned.1.call-done
  153.9 8.1 %shard_map.68 = bf16[128,8192]{1,0:T(8,128)(2,1)} custom-call(bf16[128,8192]{1,0:T(8,128)(2,1)} %input_ref.3, bf16[128,512]{1,0:T(8,128)(2,1)} %cotangent_ref.1, bf16[16,512,512]{2,1,0:T(8,128)(2,1)} %bitcast.15, f32[128,128]{1,0:T(8,128)} %get-tuple-element.11.scale_ref), custom_call_target="tpu_custom_call" | custom-call | flops 1073741824 | bytes 12582912 | tf_op jit(solution)/shard_map/pallas_call | solution.py:228
  (2 shorter events, 0.0 us)
Async XLA Ops:
  11.4 12.8 %copy-start = (bf16[512,512]{1,0:T(8,128)(2,1)S(1)}, bf16[512,512]{1,0:T(8,128)(2,1)}, u32[]{:S(2)}) copy-start(bf16[512,512]{1,0:T(8,128)(2,1)} %param.6) | copy-start | bytes 1572868
  11.4 13.0 %copy-start.1 = (f32[512]{0:T(512)S(1)}, f32[512]{0:T(512)}, u32[]{:S(2)}) copy-start(f32[512]{0:T(512)} %param.5) | copy-start | bytes 6148
  11.4 68.7 %all-to-all-start = ((bf16[16,128,512]{2,1,0:T(8,128)(2,1)}), bf16[16,128,512]{2,1,0:T(8,128)(2,1)S(1)}, u32[]{:S(2)}, u32[]{:S(2)}) async-start(bf16[16,128,512]{2,1,0:T(8,128)(2,1)} %get-tuple-element.9), calls=%async_computation | async-start | bytes 4194304 | tf_op jit(solution)/shard_map/all_to_all | solution.py:191
  23.3 64.5 %all-gather.4.cloned.1.call-start = ((), (), s32[]{:S(2)}) async-start(), calls=%async_computation.4 | async-start | bytes 2228224 | tf_op jit(solution)/shard_map/all_gather | solution.py:175
  24.1 129.8 %all-gather.6.cloned.1.call-start = ((), (), s32[]{:S(2)}) async-start(), calls=%async_computation.5 | async-start | bytes 8912896 | tf_op jit(solution)/shard_map/all_gather | solution.py:196
  91.5 26.0 %all-to-all-start.1 = ((bf16[32,16,512]{2,1,0:T(8,128)(2,1)}), bf16[32,16,512]{2,1,0:T(8,128)(2,1)S(1)}, u32[]{:S(2)}, u32[]{:S(2)}) async-start(bf16[32,16,512]{2,1,0:T(8,128)(2,1)} %bitcast.4), calls=%async_computation.1 | async-start | bytes 1048576 | tf_op jit(solution)/shard_map/all_to_all | solution.py:204
Sparse Core Ops, SparseCore 0:
  26.3 61.4 all-gather.3
  89.9 58.6 all-gather.5

commit v4 on v3

--- a/solution.py
+++ b/solution.py
@@ -12,6 +12,7 @@
 REPLICAS = 32
 LANES = 128
 PARAMS = pltpu.CompilerParams(vmem_limit_bytes=32 * 1024 * 1024)
+INPUT = pltpu.CompilerParams(vmem_limit_bytes=57 * 1024 * 1024)
 LARGE = pltpu.CompilerParams(vmem_limit_bytes=60 * 1024 * 1024)
 
 
@@ -102,7 +103,7 @@
     return weights
 
 
-def combine_kernel(packed_ref, shards_ref, parts_ref, weight_ref, gain_ref):
+def combine_kernel(packed_ref, shards_ref, parts_ref, done_ref, weight_ref, gain_ref):
     packed = jnp.sum(packed_ref[...], axis=0)
     weights_w = pair_weights(unpack_gram(packed[0:8]))
     weights_g = pair_weights(unpack_gram(packed[8:16]))
@@ -112,11 +113,10 @@
         shard = shards_ref[replica * width : (replica + 1) * width, :].astype(jnp.float32)
         total += weights_w[replica : replica + 1, :] * shard
     weight_ref[...] = total.astype(jnp.bfloat16)
-    for part in range(4):
-        piece = parts_ref[:, 8 + part, :]
-        gain_ref[:, part * LANES : (part + 1) * LANES] = jnp.sum(
-            weights_g * piece, axis=0, keepdims=True
-        ).astype(jnp.bfloat16)
+    gains = [
+        jnp.sum(weights_g * parts_ref[:, 8 + part, :], axis=0, keepdims=True) for part in range(4)
+    ]
+    gain_ref[...] = jnp.concatenate(gains, axis=1)[0].astype(jnp.bfloat16)
 
 
 def kernel_call(kernel, out_shape, *args):
@@ -138,13 +138,14 @@
         blocks_ref[owner, :, :] = normed[:, owner * width : (owner + 1) * width]
 
 
-def input_kernel(input_ref, cotangent_ref, weight_ref, scale_ref, out_ref, hat_ref, total_ref):
+def input_kernel(input_ref, cotangent_ref, weight_ref, scale_ref, out_ref, done_ref, hat_ref, total_ref):
     step, steps = pl.program_id(0), pl.num_programs(0)
     model, width = input_ref.shape[1], weight_ref.shape[2]
 
     @pl.when(step == 0)
     def _():
         total_ref[...] = jnp.zeros_like(total_ref)
+        done_ref[...] = jnp.zeros_like(done_ref)
 
     for block in range(weight_ref.shape[0]):
         hat = jnp.dot(
@@ -168,12 +169,16 @@
             ).astype(jnp.bfloat16)
 
 
+def scale_kernel(weight_ref, gain_ref, cotangent_ref, out_ref):
+    out_ref[...] = (weight_ref[...].T.astype(jnp.float32) * gain_ref[...]).astype(jnp.bfloat16)
+
+
 def body(layer_input, norm_gain, value_weight, value_cotangent):
     tokens, model = layer_input.shape
     peers, width = lax.axis_size("fsdp"), value_cotangent.shape[1]
     own = model // peers
     cotangent = lax.all_gather(value_cotangent, "fsdp", axis=0, tiled=True)
-    step = 32
+    step = 64
     blocks, scale = pl.pallas_call(
         norm_kernel,
         grid=(tokens // step,),
@@ -190,8 +195,21 @@
     )(layer_input)
     columns = lax.all_to_all(blocks, "fsdp", split_axis=0, concat_axis=0, tiled=True)
     columns = columns.reshape(peers * tokens, own)
-    weight_t = value_weight.T.astype(jnp.float32)
-    scaled_weight = (weight_t * norm_gain[None, :]).astype(jnp.bfloat16)
+    scaled_weight = pl.pallas_call(
+        scale_kernel,
+        grid=(1,),
+        in_specs=[
+            pl.BlockSpec((own, width), lambda i: (0, 0)),
+            pl.BlockSpec((1, own), lambda i: (0, 0)),
+            pl.BlockSpec((16, LANES), lambda i: (0, 0)),
+        ],
+        out_specs=pl.BlockSpec((width, own), lambda i: (0, 0)),
+        out_shape=jax.ShapeDtypeStruct((width, own), jnp.bfloat16),
+        compiler_params=LARGE,
+        cost_estimate=pl.CostEstimate(
+            flops=256 * tokens * model * width, bytes_accessed=4 * own * width, transcendentals=0
+        ),
+    )(value_weight, norm_gain[None, :], cotangent)
     scaled_weight, columns = lax.optimization_barrier((scaled_weight, columns))
     all_weight = lax.all_gather(scaled_weight, "fsdp", axis=0)
 
@@ -200,6 +218,7 @@
         cotangent, columns, (((0,), (0,)), ((), ())), preferred_element_type=jnp.float32
     )
     grad_w = (grad * (norm_gain * grad_scale)[None, :]).astype(jnp.bfloat16)
+    weight_t = value_weight.T.astype(jnp.float32)
     grad_g = (jnp.sum(grad * weight_t, axis=0, keepdims=True) * grad_scale).astype(jnp.bfloat16)
     shards = lax.all_to_all(grad_w, "dp", split_axis=0, concat_axis=0, tiled=True)
 
@@ -214,18 +233,8 @@
         gain_gram_kernel, jax.ShapeDtypeStruct((peers, 16, LANES), jnp.float32), parts
     )
     packed = lax.all_to_all(sent, "fsdp", split_axis=0, concat_axis=0, tiled=True)
-    weight_update, gain_update = kernel_call(
-        combine_kernel,
-        (
-            jax.ShapeDtypeStruct((shards.shape[0] // REPLICAS, own), jnp.bfloat16),
-            jax.ShapeDtypeStruct((1, own), jnp.bfloat16),
-        ),
-        packed,
-        shards,
-        parts,
-    )
-    group = 4
-    input_grad = pl.pallas_call(
+    group = 8
+    input_grad, done = pl.pallas_call(
         input_kernel,
         grid=(peers // group,),
         in_specs=[
@@ -234,18 +243,32 @@
             pl.BlockSpec((group, width, own), lambda i: (i, 0, 0)),
             pl.BlockSpec((tokens, LANES), lambda i: (0, 0)),
         ],
-        out_specs=pl.BlockSpec((tokens, model), lambda i: (0, 0)),
-        out_shape=jax.ShapeDtypeStruct((tokens, model), jnp.bfloat16),
+        out_specs=(
+            pl.BlockSpec((tokens, model), lambda i: (0, 0)),
+            pl.BlockSpec((8, LANES), lambda i: (0, 0)),
+        ),
+        out_shape=(
+            jax.ShapeDtypeStruct((tokens, model), jnp.bfloat16),
+            jax.ShapeDtypeStruct((8, LANES), jnp.float32),
+        ),
         scratch_shapes=[
             pltpu.VMEM((tokens, model), jnp.bfloat16),
             pltpu.VMEM((tokens, own), jnp.float32),
         ],
-        compiler_params=LARGE,
+        compiler_params=INPUT,
         cost_estimate=pl.CostEstimate(
             flops=2 * tokens * model * width, bytes_accessed=2 * model * (width + 2 * tokens), transcendentals=0
         ),
     )(layer_input, value_cotangent, all_weight, scale)
-    return (input_grad, weight_update.T, gain_update[0])
+    weight_update, gain_update = pl.pallas_call(
+        combine_kernel,
+        out_shape=(
+            jax.ShapeDtypeStruct((shards.shape[0] // REPLICAS, own), jnp.bfloat16),
+            jax.ShapeDtypeStruct((own,), jnp.bfloat16),
+        ),
+        compiler_params=PARAMS,
+    )(packed, shards, parts, done)
+    return (input_grad, weight_update.T, gain_update)
 
 
 def solution(mesh):

time: 169 us -> 163 us (0.964)
  blocking collectives: 33 us -> 15.2 us
  starting transfers between devices: 21.5 us -> 31.6 us
    all_to_all x1, waiting for transfers between devices: 54.8 us -> 0.01 us  [body(): lax.all_to_all(blocks, 'fsdp', split_axis=0, concat_axis=0, tiled=True)]
    all_gather x1, waiting for transfers between devices: 7.68 us -> 59.7 us  [body(): cotangent = lax.all_gather(value_cotangent, 'fsdp', axis=0, tiled=True)]
    all_to_all x1 -> x0, blocking collectives: 17.8 us -> none  [body(): lax.all_to_all(sent, 'fsdp', split_axis=0, concat_axis=0, tiled=True)]
    all_to_all x0 -> x1, starting transfers between devices: none -> 10.5 us  [body(): lax.all_to_all(sent, 'fsdp', split_axis=0, concat_axis=0, tiled=True)]
    pallas_call x0 -> x2, Pallas kernels: none -> 3.72 us  [the longest x1 2.1 us: body(): pl.pallas_call(scale_kernel, grid=(1,), in_specs=[pl.BlockSpec((own, widt...]
    all_gather x1, waiting for transfers between devices: 0.01 us -> 2.95 us  [body(): all_weight = lax.all_gather(scaled_weight, 'fsdp', axis=0)]
  transfers between devices with their start and end apart: 4 -> 5, of which waited for: 3 -> 3; matrix products, arithmetic and copies ran while one was open for 3% -> 2% of each run, Pallas kernels for 2% -> 9%
where the time goes in v4:
time: 163 us; the launch traced here: 161 us
  waiting for transfers between devices  79.9 us (49%)
  starting transfers between devices  31.6 us (19%)
  Pallas kernels  16 us (10%)
  blocking collectives  15.2 us (9%)
  between operations  14.1 us (9%)
  matrix products  3.71 us (2%)
    all_gather x1, waiting for transfers between devices, body(): cotangent = lax.all_gather(value_cotangent, 'fsdp', axis=0, tiled=True)  59.7 us
    all_to_all x1, waiting for transfers between devices, body(): lax.all_to_all(grad_w, 'dp', split_axis=0, concat_axis=0, tiled=True)  16.6 us
    all_to_all x1, blocking collectives, body(): parts = lax.all_to_all(sent, 'dp', split_axis=0, concat_axis=0, tiled=True)  15.2 us
    all_to_all x1, starting transfers between devices, body(): lax.all_to_all(blocks, 'fsdp', split_axis=0, concat_axis=0, tiled=True)  11.8 us
    all_to_all x1, starting transfers between devices, body(): lax.all_to_all(sent, 'fsdp', split_axis=0, concat_axis=0, tiled=True)  10.5 us
    all_to_all x1, starting transfers between devices, body(): lax.all_to_all(grad_w, 'dp', split_axis=0, concat_axis=0, tiled=True)  9.27 us
    pallas_call x1, Pallas kernels, body(): pl.pallas_call(input_kernel, grid=(peers // group,), in_specs=[pl.BlockSp...  7.43 us
    dot_general x1, matrix products, body(): lax.dot_general(cotangent, columns, (((0,), (0,)), ((), ())), preferred_e...  3.71 us
  transfers between devices with their start and end apart: 5, of which 3 were waited for; matrix products, arithmetic and copies ran while one was open for 2% of the time, Pallas kernels for 9%

profile of v4, /device:TPU:1, one launch (start us, length us, event | category | flops | bytes accessed | tf_op | source)
XLA Modules:
  0.0 161.5 jit_solution(4629950273732664952)
XLA Ops:
  7.2 0.0 all-gather.4.cloned.1.call-start
  7.2 0.7 all-gather.4.cloned.1.call-update
  7.9 3.1 %shard_map.68 = (bf16[16,128,512]{2,1,0:T(8,128)(2,1)}, f32[128,128]{1,0:T(8,128)}) custom-call(bf16[128,8192]{1,0:T(8,128)(2,1)} %input_ref.3), custom_call_target="tpu_custom_call" | custom-call | tf_op jit(solution)/shard_map/pallas_call | solution.py:182
  11.0 11.8 %all-to-all-start = ((bf16[16,128,512]{2,1,0:T(8,128)(2,1)}), bf16[16,128,512]{2,1,0:T(8,128)(2,1)S(1)}, u32[]{:S(2)}, u32[]{:S(2)}) async-start(bf16[16,128,512]{2,1,0:T(8,128)(2,1)} %get-tuple-element.11), calls=%async_computation | async-start | bytes 4194304 | tf_op jit(solution)/shard_map/all_to_all | solution.py:196
  22.9 0.0 all-gather.6.cloned.1.call-start
  22.9 59.7 %all-gather.4.cloned.1.call-done.cotangent_ref = bf16[2048,512]{1,0:T(8,128)(2,1)} async-done(((bf16[128,512]{1,0:T(8,128)(2,1)}), bf16[2048,512]{1,0:T(8,128)(2,1)}) %all-gather.4.cloned.1.call-update) | async-done | bytes 2097168 | tf_op jit(solution)/shard_map/all_gather | solution.py:180
  82.6 0.0 copy-start.1
  82.6 0.0 copy-start.2
  82.6 2.1 %shard_map.67 = bf16[512,512]{1,0:T(8,128)(2,1)} custom-call(bf16[512,512]{1,0:T(8,128)(2,1)} %weight_ref.1, f32[1,512]{1,0:T(1,128)} %bitcast.16, bf16[2048,512]{1,0:T(8,128)(2,1)} %all-gather.4.cloned.1.call-done.cotangent_ref), custom_call_target="tpu_custom_call" | custom-call | flops 137438953472 | bytes 1048576 | tf_op jit(solution)/shard_map/pallas_call | solution.py:198
  84.7 0.0 all-to-all-done
  84.7 0.0 all-gather.6.cloned.1.call-update
  84.8 0.0 copy-done.1
  84.8 0.2 copy.7
  85.0 0.0 copy-done.2
  85.0 3.7 %multiply_reduce_fusion = (f32[512]{0:T(512)S(1)}, bf16[512,512]{0,1:T(8,128)(2,1)}) fusion(bf16[512,512]{0,1:T(8,128)(2,1)S(1)} %copy.7, f32[512]{0:T(512)S(1)} %broadcast_multiply_fusion, bf16[2048,512]{1,0:T(8,128)(2,1)S(1)} %bitcast.15, bf16[2048,512]{1,0:T(8,128)(2,1)} %all-gather.4.cloned.1.call-done.cotangent_ref), kind=kOutput, calls=%fused_computation | convolution fusion | flops 1075052032 | bytes 5246976 | tf_op jit(solution)/shard_map/dot_general | solution.py:217
  88.7 9.3 %all-to-all-start.1 = ((bf16[32,16,512]{2,1,0:T(8,128)(2,1)}), bf16[32,16,512]{2,1,0:T(8,128)(2,1)S(1)}, u32[]{:S(2)}, u32[]{:S(2)}) async-start(bf16[32,16,512]{2,1,0:T(8,128)(2,1)} %bitcast.4), calls=%async_computation.1 | async-start | bytes 1048576 | tf_op jit(solution)/shard_map/all_to_all | solution.py:223
  98.0 16.6 %all-to-all-done.1 = bf16[32,16,512]{2,1,0:T(8,128)(2,1)S(1)} async-done(((bf16[32,16,512]{2,1,0:T(8,128)(2,1)}), bf16[32,16,512]{2,1,0:T(8,128)(2,1)S(1)}, u32[]{:S(2)}, u32[]{:S(2)}) %all-to-all-start.1) | async-done | bytes 524320 | tf_op jit(solution)/shard_map/all_to_all | solution.py:223
  114.6 0.8 shard_map.70
  115.4 15.2 %all_to_all.26.parts_ref = f32[32,16,128]{2,1,0:T(8,128)S(1)} all-to-all(f32[32,16,128]{2,1,0:T(8,128)S(1)} %shard_map.70), channel_id=1, replica_groups=mesh['dp'=32,'fsdp'=16] {'dp'}, dimensions={0} | all-to-all | bytes 524288 | tf_op jit(solution)/shard_map/all_to_all | solution.py:231
  130.6 0.9 shard_map.71
  131.5 10.5 %all-to-all-start.3 = ((f32[16,16,128]{2,1,0:T(8,128)}), f32[16,16,128]{2,1,0:T(8,128)S(1)}, u32[]{:S(2)}, u32[]{:S(2)}) async-start(f32[16,16,128]{2,1,0:T(8,128)} %shard_map.71), calls=%async_computation.3 | async-start | bytes 262144 | tf_op jit(solution)/shard_map/all_to_all | solution.py:235
  142.0 2.9 %all-gather.6.cloned.1.call-done = bf16[8192,512]{1,0:T(8,128)(2,1)} async-done(((bf16[512,512]{1,0:T(8,128)(2,1)}), bf16[8192,512]{1,0:T(8,128)(2,1)}) %all-gather.6.cloned.1.call-update) | async-done | bytes 8388624 | tf_op jit(solution)/shard_map/all_gather | solution.py:214
  144.9 7.4 %shard_map.69 = (bf16[128,8192]{1,0:T(8,128)(2,1)}, f32[8,128]{1,0:T(8,128)}) custom-call(bf16[128,8192]{1,0:T(8,128)(2,1)} %input_ref.3, bf16[128,512]{1,0:T(8,128)(2,1)} %cotangent_ref.1, bf16[16,512,512]{2,1,0:T(8,128)(2,1)} %bitcast.14, f32[128,128]{1,0:T(8,128)} %get-tuple-element.13.scale_ref), custom_call_target="tpu_custom_call" | custom-call | flops 1073741824 | bytes 12582912 | tf_op jit(solution)/shard_map/pallas_call | solution.py:237
  152.3 0.0 all-to-all-done.3.packed_ref
  152.3 0.0 copy-start
  152.3 0.7 copy-done
  153.0 1.6 %shard_map.72 = (bf16[16,512]{1,0:T(8,128)(2,1)}, bf16[512]{0:T(512)(128)(2,1)}) custom-call(f32[16,16,128]{2,1,0:T(8,128)S(1)} %all-to-all-done.3.packed_ref, bf16[512,512]{1,0:T(8,128)(2,1)S(1)} %bitcast.12, f32[32,16,128]{2,1,0:T(8,128)S(1)} %all_to_all.26.parts_ref, f32[8,128]{1,0:T(8,128)S(1)} %copy-done), custom_call_target="tpu_custom_call" | custom-call | tf_op jit(solution)/shard_map/pallas_call | solution.py:263
  (2 shorter events, 0.0 us)
Async XLA Ops:
  7.2 75.5 %all-gather.4.cloned.1.call-start = ((), (), s32[]{:S(2)}) async-start(), calls=%async_computation.4 | async-start | bytes 2228224 | tf_op jit(solution)/shard_map/all_gather | solution.py:180
  11.0 73.7 %all-to-all-start = ((bf16[16,128,512]{2,1,0:T(8,128)(2,1)}), bf16[16,128,512]{2,1,0:T(8,128)(2,1)S(1)}, u32[]{:S(2)}, u32[]{:S(2)}) async-start(bf16[16,128,512]{2,1,0:T(8,128)(2,1)} %get-tuple-element.11), calls=%async_computation | async-start | bytes 4194304 | tf_op jit(solution)/shard_map/all_to_all | solution.py:196
  22.9 122.0 %all-gather.6.cloned.1.call-start = ((), (), s32[]{:S(2)}) async-start(), calls=%async_computation.5 | async-start | bytes 8912896 | tf_op jit(solution)/shard_map/all_gather | solution.py:214
  82.6 2.1 %copy-start.1 = (bf16[512,512]{1,0:T(8,128)(2,1)S(1)}, bf16[512,512]{1,0:T(8,128)(2,1)}, u32[]{:S(2)}) copy-start(bf16[512,512]{1,0:T(8,128)(2,1)} %weight_ref.1) | copy-start | bytes 1572868
  82.6 2.4 %copy-start.2 = (f32[512]{0:T(512)S(1)}, f32[512]{0:T(512)}, u32[]{:S(2)}) copy-start(f32[512]{0:T(512)} %param.5) | copy-start | bytes 6148
  88.7 25.9 %all-to-all-start.1 = ((bf16[32,16,512]{2,1,0:T(8,128)(2,1)}), bf16[32,16,512]{2,1,0:T(8,128)(2,1)S(1)}, u32[]{:S(2)}, u32[]{:S(2)}) async-start(bf16[32,16,512]{2,1,0:T(8,128)(2,1)} %bitcast.4), calls=%async_computation.1 | async-start | bytes 1048576 | tf_op jit(solution)/shard_map/all_to_all | solution.py:223
  131.5 20.8 %all-to-all-start.3 = ((f32[16,16,128]{2,1,0:T(8,128)}), f32[16,16,128]{2,1,0:T(8,128)S(1)}, u32[]{:S(2)}, u32[]{:S(2)}) async-start(f32[16,16,128]{2,1,0:T(8,128)} %shard_map.71), calls=%async_computation.3 | async-start | bytes 262144 | tf_op jit(solution)/shard_map/all_to_all | solution.py:235
  152.3 0.7 copy-start
Sparse Core Ops, SparseCore 0:
  10.1 72.4 all-gather.3
  84.9 59.9 all-gather.5

commit v5 on v4

--- a/solution.py
+++ b/solution.py
@@ -11,8 +11,8 @@
 EPS_SUM = 1e-06
 REPLICAS = 32
 LANES = 128
+CHUNKS = 4
 PARAMS = pltpu.CompilerParams(vmem_limit_bytes=32 * 1024 * 1024)
-INPUT = pltpu.CompilerParams(vmem_limit_bytes=57 * 1024 * 1024)
 LARGE = pltpu.CompilerParams(vmem_limit_bytes=60 * 1024 * 1024)
 
 
@@ -138,39 +138,82 @@
         blocks_ref[owner, :, :] = normed[:, owner * width : (owner + 1) * width]
 
 
-def input_kernel(input_ref, cotangent_ref, weight_ref, scale_ref, out_ref, done_ref, hat_ref, total_ref):
-    step, steps = pl.program_id(0), pl.num_programs(0)
-    model, width = input_ref.shape[1], weight_ref.shape[2]
-
-    @pl.when(step == 0)
-    def _():
-        total_ref[...] = jnp.zeros_like(total_ref)
-        done_ref[...] = jnp.zeros_like(done_ref)
-
-    for block in range(weight_ref.shape[0]):
-        hat = jnp.dot(
-            cotangent_ref[...], weight_ref[block], preferred_element_type=jnp.float32
-        ).astype(jnp.bfloat16)
-        at = (step * weight_ref.shape[0] + block) * width
-        columns = pl.ds(pl.multiple_of(at, width), width)
+def input_kernel(
+    input_hbm,
+    cotangent_hbm,
+    weight_hbm,
+    scale_hbm,
+    out_hbm,
+    done_hbm,
+    input_ref,
+    cotangent_ref,
+    weight_ref,
+    scale_ref,
+    hat_ref,
+    out_ref,
+    input_sem,
+    small_sem,
+    weight_sem,
+    out_sem,
+):
+    blocks, width = weight_ref.shape[0], weight_ref.shape[2]
+    chunk = blocks // CHUNKS
+    small = [
+        pltpu.make_async_copy(cotangent_hbm, cotangent_ref, small_sem.at[0]),
+        pltpu.make_async_copy(scale_hbm, scale_ref, small_sem.at[1]),
+    ]
+    small[0].start()
+    arriving = []
+    for part in range(CHUNKS):
+        at = pl.ds(part * chunk, chunk)
+        columns = pl.ds(part * chunk * width, chunk * width)
+        pair = [
+            pltpu.make_async_copy(weight_hbm.at[at], weight_ref.at[at], weight_sem.at[part]),
+            pltpu.make_async_copy(
+                input_hbm.at[:, columns], input_ref.at[:, columns], input_sem.at[part]
+            ),
+        ]
+        for copy in pair:
+            copy.start()
+        arriving.append(pair)
+    small[1].start()
+    small[0].wait()
+    cotangent = cotangent_ref[...]
+    total = jnp.zeros((cotangent.shape[0], LANES), jnp.float32)
+    for block in range(blocks):
+        if block % chunk == 0:
+            for copy in arriving[block // chunk]:
+                copy.wait()
+        columns = slice(block * width, (block + 1) * width)
+        hat = jnp.dot(cotangent, weight_ref[block], preferred_element_type=jnp.float32).astype(
+            jnp.bfloat16
+        )
         hat_ref[:, columns] = hat
-        total_ref[...] += hat.astype(jnp.float32) * input_ref[:, columns].astype(jnp.float32)
-
-    @pl.when(step == steps - 1)
-    def _():
-        inverse_rms = scale_ref[:, 0:1]
-        factor = jnp.sum(total_ref[...], axis=1, keepdims=True) / model
-        factor = inverse_rms * inverse_rms * factor
-        for part in range(model // width):
-            at = slice(part * width, (part + 1) * width)
-            piece = input_ref[:, at].astype(jnp.float32)
-            out_ref[:, at] = (
-                inverse_rms * (hat_ref[:, at].astype(jnp.float32) - piece * factor)
+        terms = hat.astype(jnp.float32) * input_ref[:, columns].astype(jnp.float32)
+        for lane in range(0, width, LANES):
+            total += terms[:, lane : lane + LANES]
+    small[1].wait()
+    inverse_rms = scale_ref[:, 0:1]
+    factor = jnp.sum(total, axis=1, keepdims=True) / (blocks * width)
+    factor = inverse_rms * inverse_rms * factor
+    leaving = []
+    for part in range(CHUNKS):
+        for block in range(part * chunk, (part + 1) * chunk):
+            columns = slice(block * width, (block + 1) * width)
+            piece = input_ref[:, columns].astype(jnp.float32)
+            out_ref[:, columns] = (
+                inverse_rms * (hat_ref[:, columns].astype(jnp.float32) - piece * factor)
             ).astype(jnp.bfloat16)
-
-
-def scale_kernel(weight_ref, gain_ref, cotangent_ref, out_ref):
-    out_ref[...] = (weight_ref[...].T.astype(jnp.float32) * gain_ref[...]).astype(jnp.bfloat16)
+        at = pl.ds(part * chunk * width, chunk * width)
+        copy = pltpu.make_async_copy(out_ref.at[:, at], out_hbm.at[:, at], out_sem.at[part])
+        copy.start()
+        leaving.append(copy)
+    for copy in leaving:
+        copy.wait()
+
+
+def gate_kernel(value_ref, after_ref, out_ref):
+    pass
 
 
 def body(layer_input, norm_gain, value_weight, value_cotangent):
@@ -195,21 +238,20 @@
     )(layer_input)
     columns = lax.all_to_all(blocks, "fsdp", split_axis=0, concat_axis=0, tiled=True)
     columns = columns.reshape(peers * tokens, own)
+    weight_t = value_weight.T.astype(jnp.float32)
+    scaled_weight = (weight_t * norm_gain[None, :]).astype(jnp.bfloat16)
+    hbm = pl.BlockSpec(memory_space=pltpu.HBM)
     scaled_weight = pl.pallas_call(
-        scale_kernel,
-        grid=(1,),
-        in_specs=[
-            pl.BlockSpec((own, width), lambda i: (0, 0)),
-            pl.BlockSpec((1, own), lambda i: (0, 0)),
-            pl.BlockSpec((16, LANES), lambda i: (0, 0)),
-        ],
-        out_specs=pl.BlockSpec((width, own), lambda i: (0, 0)),
+        gate_kernel,
+        in_specs=[hbm, hbm],
+        out_specs=hbm,
         out_shape=jax.ShapeDtypeStruct((width, own), jnp.bfloat16),
+        input_output_aliases={0: 0},
         compiler_params=LARGE,
         cost_estimate=pl.CostEstimate(
             flops=256 * tokens * model * width, bytes_accessed=4 * own * width, transcendentals=0
         ),
-    )(value_weight, norm_gain[None, :], cotangent)
+    )(scaled_weight, cotangent)
     scaled_weight, columns = lax.optimization_barrier((scaled_weight, columns))
     all_weight = lax.all_gather(scaled_weight, "fsdp", axis=0)
 
@@ -218,7 +260,6 @@
         cotangent, columns, (((0,), (0,)), ((), ())), preferred_element_type=jnp.float32
     )
     grad_w = (grad * (norm_gain * grad_scale)[None, :]).astype(jnp.bfloat16)
-    weight_t = value_weight.T.astype(jnp.float32)
     grad_g = (jnp.sum(grad * weight_t, axis=0, keepdims=True) * grad_scale).astype(jnp.bfloat16)
     shards = lax.all_to_all(grad_w, "dp", split_axis=0, concat_axis=0, tiled=True)
 
@@ -233,35 +274,35 @@
         gain_gram_kernel, jax.ShapeDtypeStruct((peers, 16, LANES), jnp.float32), parts
     )
     packed = lax.all_to_all(sent, "fsdp", split_axis=0, concat_axis=0, tiled=True)
-    group = 8
+    vmem = pl.BlockSpec(memory_space=pltpu.VMEM)
     input_grad, done = pl.pallas_call(
         input_kernel,
-        grid=(peers // group,),
-        in_specs=[
-            pl.BlockSpec((tokens, model), lambda i: (0, 0)),
-            pl.BlockSpec((tokens, width), lambda i: (0, 0)),
-            pl.BlockSpec((group, width, own), lambda i: (i, 0, 0)),
-            pl.BlockSpec((tokens, LANES), lambda i: (0, 0)),
-        ],
-        out_specs=(
-            pl.BlockSpec((tokens, model), lambda i: (0, 0)),
-            pl.BlockSpec((8, LANES), lambda i: (0, 0)),
-        ),
+        in_specs=[hbm, hbm, hbm, hbm],
+        out_specs=(hbm, hbm),
         out_shape=(
             jax.ShapeDtypeStruct((tokens, model), jnp.bfloat16),
             jax.ShapeDtypeStruct((8, LANES), jnp.float32),
         ),
         scratch_shapes=[
             pltpu.VMEM((tokens, model), jnp.bfloat16),
-            pltpu.VMEM((tokens, own), jnp.float32),
+            pltpu.VMEM((tokens, width), jnp.bfloat16),
+            pltpu.VMEM((peers, width, own), jnp.bfloat16),
+            pltpu.VMEM((tokens, LANES), jnp.float32),
+            pltpu.VMEM((tokens, model), jnp.bfloat16),
+            pltpu.VMEM((tokens, model), jnp.bfloat16),
+            pltpu.SemaphoreType.DMA((CHUNKS,)),
+            pltpu.SemaphoreType.DMA((2,)),
+            pltpu.SemaphoreType.DMA((CHUNKS,)),
+            pltpu.SemaphoreType.DMA((CHUNKS,)),
         ],
-        compiler_params=INPUT,
+        compiler_params=LARGE,
         cost_estimate=pl.CostEstimate(
             flops=2 * tokens * model * width, bytes_accessed=2 * model * (width + 2 * tokens), transcendentals=0
         ),
     )(layer_input, value_cotangent, all_weight, scale)
     weight_update, gain_update = pl.pallas_call(
         combine_kernel,
+        in_specs=[vmem, vmem, vmem, hbm],
         out_shape=(
             jax.ShapeDtypeStruct((shards.shape[0] // REPLICAS, own), jnp.bfloat16),
             jax.ShapeDtypeStruct((own,), jnp.bfloat16),

time: 163 us -> 162 us (level)
  Pallas kernels: 16 us -> 12.9 us
    pallas_call x3, Pallas kernels: 11.2 us -> 8.05 us  [the longest x1 6.43 us: body(): pl.pallas_call(input_kernel, in_specs=[hbm, hbm, hbm, hbm], out_specs=(hb...]
    all_gather x1, waiting for transfers between devices: 2.95 us -> 5.16 us  [body(): all_weight = lax.all_gather(scaled_weight, 'fsdp', axis=0)]
    all_gather x1, waiting for transfers between devices: 59.7 us -> 58.1 us  [body(): cotangent = lax.all_gather(value_cotangent, 'fsdp', axis=0, tiled=True)]
  transfers between devices with their start and end apart: 5 -> 5, of which waited for: 3 -> 3; matrix products, arithmetic and copies ran while one was open for 2% -> 3% of each run, Pallas kernels for 9% -> 7%
where the time goes in v5:
time: 162 us; the launch traced here: 160 us
  waiting for transfers between devices  80.5 us (50%)
  starting transfers between devices  32.1 us (20%)
  blocking collectives  15.2 us (9%)
  between operations  14.1 us (9%)
  Pallas kernels  12.9 us (8%)
  matrix products  3.72 us (2%)
    all_gather x1, waiting for transfers between devices, body(): cotangent = lax.all_gather(value_cotangent, 'fsdp', axis=0, tiled=True)  58.1 us
    all_to_all x1, waiting for transfers between devices, body(): lax.all_to_all(grad_w, 'dp', split_axis=0, concat_axis=0, tiled=True)  16.6 us
    all_to_all x1, blocking collectives, body(): parts = lax.all_to_all(sent, 'dp', split_axis=0, concat_axis=0, tiled=True)  15.2 us
    all_to_all x1, starting transfers between devices, body(): lax.all_to_all(blocks, 'fsdp', split_axis=0, concat_axis=0, tiled=True)  12 us
    all_to_all x1, starting transfers between devices, body(): lax.all_to_all(sent, 'fsdp', split_axis=0, concat_axis=0, tiled=True)  10.5 us
    all_to_all x1, starting transfers between devices, body(): lax.all_to_all(grad_w, 'dp', split_axis=0, concat_axis=0, tiled=True)  9.59 us
    pallas_call x1, Pallas kernels, body(): pl.pallas_call(input_kernel, in_specs=[hbm, hbm, hbm, hbm], out_specs=(hb...  6.43 us
    all_gather x1, waiting for transfers between devices, body(): all_weight = lax.all_gather(scaled_weight, 'fsdp', axis=0)  5.16 us
  transfers between devices with their start and end apart: 5, of which 3 were waited for; matrix products, arithmetic and copies ran while one was open for 3% of the time, Pallas kernels for 7%

profile of v5, /device:TPU:1, one launch (start us, length us, event | category | flops | bytes accessed | tf_op | source)
XLA Modules:
  0.0 160.3 jit_solution(16625100094372851349)
XLA Ops:
  7.2 0.0 all-gather.4.cloned.1.call-start
  7.2 0.7 all-gather.4.cloned.1.call-update
  7.9 3.1 %shard_map.68 = (bf16[16,128,512]{2,1,0:T(8,128)(2,1)}, f32[128,128]{1,0:T(8,128)}) custom-call(bf16[128,8192]{1,0:T(8,128)(2,1)} %input_hbm.1), custom_call_target="tpu_custom_call" | custom-call | tf_op jit(solution)/shard_map/pallas_call | solution.py:225
  11.0 0.0 copy-start.1
  11.0 0.0 copy-start.2
  11.0 12.0 %all-to-all-start = ((bf16[16,128,512]{2,1,0:T(8,128)(2,1)}), bf16[16,128,512]{2,1,0:T(8,128)(2,1)S(1)}, u32[]{:S(2)}, u32[]{:S(2)}) async-start(bf16[16,128,512]{2,1,0:T(8,128)(2,1)} %get-tuple-element.11), calls=%async_computation | async-start | bytes 4194304 | tf_op jit(solution)/shard_map/all_to_all | solution.py:239
  23.0 0.0 all-gather.6.cloned.1.call-start
  23.1 0.0 copy-done.1
  23.1 0.2 copy.8
  23.3 0.0 copy-done.2
  23.3 0.9 fusion.2.value_ref
  24.2 58.1 %all-gather.4.cloned.1.call-done.after_ref = bf16[2048,512]{1,0:T(8,128)(2,1)} async-done(((bf16[128,512]{1,0:T(8,128)(2,1)}), bf16[2048,512]{1,0:T(8,128)(2,1)}) %all-gather.4.cloned.1.call-update) | async-done | bytes 2097168 | tf_op jit(solution)/shard_map/all_gather | solution.py:223
  82.3 0.0 all-to-all-done
  82.3 0.0 all-gather.6.cloned.1.call-update
  82.3 3.7 %fusion.1 = (f32[512]{0:T(512)S(1)}, bf16[512,512]{0,1:T(8,128)(2,1)}) fusion(bf16[512,512]{0,1:T(8,128)(2,1)S(1)} %copy.8, f32[512]{0:T(512)S(1)} %broadcast_multiply_fusion, bf16[2048,512]{1,0:T(8,128)(2,1)S(1)} %bitcast.16, bf16[2048,512]{1,0:T(8,128)(2,1)} %all-gather.4.cloned.1.call-done.after_ref), kind=kOutput, calls=%fused_computation.3 | convolution fusion | flops 1075052032 | bytes 5246976 | tf_op jit(solution)/shard_map/dot_general | solution.py:259
  86.0 9.6 %all-to-all-start.1 = ((bf16[32,16,512]{2,1,0:T(8,128)(2,1)}), bf16[32,16,512]{2,1,0:T(8,128)(2,1)S(1)}, u32[]{:S(2)}, u32[]{:S(2)}) async-start(bf16[32,16,512]{2,1,0:T(8,128)(2,1)} %bitcast.4), calls=%async_computation.1 | async-start | bytes 1048576 | tf_op jit(solution)/shard_map/all_to_all | solution.py:264
  95.6 16.6 %all-to-all-done.1 = bf16[32,16,512]{2,1,0:T(8,128)(2,1)S(1)} async-done(((bf16[32,16,512]{2,1,0:T(8,128)(2,1)}), bf16[32,16,512]{2,1,0:T(8,128)(2,1)S(1)}, u32[]{:S(2)}, u32[]{:S(2)}) %all-to-all-start.1) | async-done | bytes 524320 | tf_op jit(solution)/shard_map/all_to_all | solution.py:264
  112.2 0.8 shard_map.70
  113.0 15.2 %all_to_all.26.parts_ref = f32[32,16,128]{2,1,0:T(8,128)S(1)} all-to-all(f32[32,16,128]{2,1,0:T(8,128)S(1)} %shard_map.70), channel_id=1, replica_groups=mesh['dp'=32,'fsdp'=16] {'dp'}, dimensions={0} | all-to-all | bytes 524288 | tf_op jit(solution)/shard_map/all_to_all | solution.py:272
  128.2 0.9 shard_map.71
  129.1 10.5 %all-to-all-start.3 = ((f32[16,16,128]{2,1,0:T(8,128)}), f32[16,16,128]{2,1,0:T(8,128)S(1)}, u32[]{:S(2)}, u32[]{:S(2)}) async-start(f32[16,16,128]{2,1,0:T(8,128)} %shard_map.71), calls=%async_computation.3 | async-start | bytes 262144 | tf_op jit(solution)/shard_map/all_to_all | solution.py:276
  139.6 5.2 %all-gather.6.cloned.1.call-done = bf16[8192,512]{1,0:T(8,128)(2,1)} async-done(((bf16[512,512]{1,0:T(8,128)(2,1)}), bf16[8192,512]{1,0:T(8,128)(2,1)}) %all-gather.6.cloned.1.call-update) | async-done | bytes 8388624 | tf_op jit(solution)/shard_map/all_gather | solution.py:256
  144.7 6.4 %shard_map.69 = (bf16[128,8192]{1,0:T(8,128)(2,1)}, f32[8,128]{1,0:T(8,128)}) custom-call(bf16[128,8192]{1,0:T(8,128)(2,1)} %input_hbm.1, bf16[128,512]{1,0:T(8,128)(2,1)} %cotangent_hbm.1, bf16[16,512,512]{2,1,0:T(8,128)(2,1)} %bitcast.15, f32[128,128]{1,0:T(8,128)} %get-tuple-element.13.scale_hbm), custom_call_target="tpu_custom_call" | custom-call | flops 1073741824 | bytes 12582912 | tf_op jit(solution)/shard_map/pallas_call | solution.py:278
  151.2 0.0 all-to-all-done.3.packed_ref
  151.2 0.0 copy-start
  151.2 0.7 copy-done
  151.9 1.6 %shard_map.72 = (bf16[16,512]{1,0:T(8,128)(2,1)}, bf16[512]{0:T(512)(128)(2,1)}) custom-call(f32[16,16,128]{2,1,0:T(8,128)S(1)} %all-to-all-done.3.packed_ref, bf16[512,512]{1,0:T(8,128)(2,1)S(1)} %bitcast.13, f32[32,16,128]{2,1,0:T(8,128)S(1)} %all_to_all.26.parts_ref, f32[8,128]{1,0:T(8,128)S(1)} %copy-done), custom_call_target="tpu_custom_call" | custom-call | tf_op jit(solution)/shard_map/pallas_call | solution.py:303
  (3 shorter events, 0.0 us)
Async XLA Ops:
  7.2 75.1 %all-gather.4.cloned.1.call-start = ((), (), s32[]{:S(2)}) async-start(), calls=%async_computation.4 | async-start | bytes 2228224 | tf_op jit(solution)/shard_map/all_gather | solution.py:223
  11.0 12.0 %copy-start.1 = (bf16[512,512]{1,0:T(8,128)(2,1)S(1)}, bf16[512,512]{1,0:T(8,128)(2,1)}, u32[]{:S(2)}) copy-start(bf16[512,512]{1,0:T(8,128)(2,1)} %param.6) | copy-start | bytes 1572868
  11.0 12.2 %copy-start.2 = (f32[512]{0:T(512)S(1)}, f32[512]{0:T(512)}, u32[]{:S(2)}) copy-start(f32[512]{0:T(512)} %param.5) | copy-start | bytes 6148
  11.0 71.2 %all-to-all-start = ((bf16[16,128,512]{2,1,0:T(8,128)(2,1)}), bf16[16,128,512]{2,1,0:T(8,128)(2,1)S(1)}, u32[]{:S(2)}, u32[]{:S(2)}) async-start(bf16[16,128,512]{2,1,0:T(8,128)(2,1)} %get-tuple-element.11), calls=%async_computation | async-start | bytes 4194304 | tf_op jit(solution)/shard_map/all_to_all | solution.py:239
  23.0 121.7 %all-gather.6.cloned.1.call-start = ((), (), s32[]{:S(2)}) async-start(), calls=%async_computation.5 | async-start | bytes 8912896 | tf_op jit(solution)/shard_map/all_gather | solution.py:256
  86.0 26.2 %all-to-all-start.1 = ((bf16[32,16,512]{2,1,0:T(8,128)(2,1)}), bf16[32,16,512]{2,1,0:T(8,128)(2,1)S(1)}, u32[]{:S(2)}, u32[]{:S(2)}) async-start(bf16[32,16,512]{2,1,0:T(8,128)(2,1)} %bitcast.4), calls=%async_computation.1 | async-start | bytes 1048576 | tf_op jit(solution)/shard_map/all_to_all | solution.py:264
  129.1 22.1 %all-to-all-start.3 = ((f32[16,16,128]{2,1,0:T(8,128)}), f32[16,16,128]{2,1,0:T(8,128)S(1)}, u32[]{:S(2)}, u32[]{:S(2)}) async-start(f32[16,16,128]{2,1,0:T(8,128)} %shard_map.71), calls=%async_computation.3 | async-start | bytes 262144 | tf_op jit(solution)/shard_map/all_to_all | solution.py:276
  151.2 0.7 copy-start
Sparse Core Ops, SparseCore 0:
  10.1 72.1 all-gather.3
  84.4 60.2 all-gather.5

commit v6 on v5

--- a/solution.py
+++ b/solution.py
@@ -103,7 +103,7 @@
     return weights
 
 
-def combine_kernel(packed_ref, shards_ref, parts_ref, done_ref, weight_ref, gain_ref):
+def combine_kernel(packed_ref, shards_ref, parts_ref, weight_ref, gain_ref):
     packed = jnp.sum(packed_ref[...], axis=0)
     weights_w = pair_weights(unpack_gram(packed[0:8]))
     weights_g = pair_weights(unpack_gram(packed[8:16]))
@@ -144,7 +144,6 @@
     weight_hbm,
     scale_hbm,
     out_hbm,
-    done_hbm,
     input_ref,
     cotangent_ref,
     weight_ref,
@@ -274,15 +273,11 @@
         gain_gram_kernel, jax.ShapeDtypeStruct((peers, 16, LANES), jnp.float32), parts
     )
     packed = lax.all_to_all(sent, "fsdp", split_axis=0, concat_axis=0, tiled=True)
-    vmem = pl.BlockSpec(memory_space=pltpu.VMEM)
-    input_grad, done = pl.pallas_call(
+    input_grad = pl.pallas_call(
         input_kernel,
         in_specs=[hbm, hbm, hbm, hbm],
-        out_specs=(hbm, hbm),
-        out_shape=(
-            jax.ShapeDtypeStruct((tokens, model), jnp.bfloat16),
-            jax.ShapeDtypeStruct((8, LANES), jnp.float32),
-        ),
+        out_specs=hbm,
+        out_shape=jax.ShapeDtypeStruct((tokens, model), jnp.bfloat16),
         scratch_shapes=[
             pltpu.VMEM((tokens, model), jnp.bfloat16),
             pltpu.VMEM((tokens, width), jnp.bfloat16),
@@ -302,13 +297,12 @@
     )(layer_input, value_cotangent, all_weight, scale)
     weight_update, gain_update = pl.pallas_call(
         combine_kernel,
-        in_specs=[vmem, vmem, vmem, hbm],
         out_shape=(
             jax.ShapeDtypeStruct((shards.shape[0] // REPLICAS, own), jnp.bfloat16),
             jax.ShapeDtypeStruct((own,), jnp.bfloat16),
         ),
         compiler_params=PARAMS,
-    )(packed, shards, parts, done)
+    )(packed, shards, parts)
     return (input_grad, weight_update.T, gain_update)
 
 

time: 162 us -> 163 us (level)
  blocking collectives: 15.2 us -> 34.6 us
  starting transfers between devices: 32.1 us -> 21.6 us
  waiting for transfers between devices: 80.5 us -> 75.4 us
    all_to_all x0 -> x1, blocking collectives: none -> 19.4 us  [body(): lax.all_to_all(sent, 'fsdp', split_axis=0, concat_axis=0, tiled=True)]
    all_to_all x1 -> x0, starting transfers between devices: 10.5 us -> none  [body(): lax.all_to_all(sent, 'fsdp', split_axis=0, concat_axis=0, tiled=True)]
    all_gather x1, waiting for transfers between devices: 5.16 us -> 0.01 us  [body(): all_weight = lax.all_gather(scaled_weight, 'fsdp', axis=0)]
  transfers between devices with their start and end apart: 5 -> 4, of which waited for: 3 -> 2; matrix products, arithmetic and copies ran while one was open for 3% -> 3% of each run, Pallas kernels for 7% -> 4%
where the time goes in v6:
time: 163 us
  waiting for transfers between devices  75.4 us (46%)
  blocking collectives  34.6 us (21%)
  starting transfers between devices  21.6 us (13%)
  between operations  14.1 us (9%)
  Pallas kernels  12.3 us (8%)
  matrix products  3.72 us (2%)
    all_gather x1, waiting for transfers between devices, body(): cotangent = lax.all_gather(value_cotangent, 'fsdp', axis=0, tiled=True)  58.1 us
    all_to_all x1, blocking collectives, body(): lax.all_to_all(sent, 'fsdp', split_axis=0, concat_axis=0, tiled=True)  19.4 us
    all_to_all x1, waiting for transfers between devices, body(): lax.all_to_all(grad_w, 'dp', split_axis=0, concat_axis=0, tiled=True)  16.6 us
    all_to_all x1, blocking collectives, body(): parts = lax.all_to_all(sent, 'dp', split_axis=0, concat_axis=0, tiled=True)  15.2 us
    all_to_all x1, starting transfers between devices, body(): lax.all_to_all(blocks, 'fsdp', split_axis=0, concat_axis=0, tiled=True)  12 us
    all_to_all x1, starting transfers between devices, body(): lax.all_to_all(grad_w, 'dp', split_axis=0, concat_axis=0, tiled=True)  9.59 us
    pallas_call x1, Pallas kernels, body(): pl.pallas_call(input_kernel, in_specs=[hbm, hbm, hbm, hbm], out_specs=hbm...  6.43 us
    dot_general x1, matrix products, body(): lax.dot_general(cotangent, columns, (((0,), (0,)), ((), ())), preferred_e...  3.72 us
  transfers between devices with their start and end apart: 4, of which 2 were waited for; matrix products, arithmetic and copies ran while one was open for 3% of the time, Pallas kernels for 4%

profile of v6, /device:TPU:1, one launch (start us, length us, event | category | flops | bytes accessed | tf_op | source)
XLA Modules:
  0.0 162.8 jit_solution(5183656611698778553)
XLA Ops:
  7.2 0.0 all-gather.4.cloned.1.call-start
  7.2 0.7 all-gather.4.cloned.1.call-update
  7.9 3.1 %shard_map.68 = (bf16[16,128,512]{2,1,0:T(8,128)(2,1)}, f32[128,128]{1,0:T(8,128)}) custom-call(bf16[128,8192]{1,0:T(8,128)(2,1)} %input_hbm.1), custom_call_target="tpu_custom_call" | custom-call | tf_op jit(solution)/shard_map/pallas_call | solution.py:224
  11.0 0.0 copy-start
  11.0 0.0 copy-start.1
  11.0 12.0 %all-to-all-start = ((bf16[16,128,512]{2,1,0:T(8,128)(2,1)}), bf16[16,128,512]{2,1,0:T(8,128)(2,1)S(1)}, u32[]{:S(2)}, u32[]{:S(2)}) async-start(bf16[16,128,512]{2,1,0:T(8,128)(2,1)} %get-tuple-element.9), calls=%async_computation | async-start | bytes 4194304 | tf_op jit(solution)/shard_map/all_to_all | solution.py:238
  23.0 0.0 all-gather.6.cloned.1.call-start
  23.1 0.0 copy-done
  23.1 0.2 copy.8
  23.3 0.0 copy-done.1
  23.3 0.9 fusion.2.value_ref
  24.2 58.1 %all-gather.4.cloned.1.call-done.after_ref = bf16[2048,512]{1,0:T(8,128)(2,1)} async-done(((bf16[128,512]{1,0:T(8,128)(2,1)}), bf16[2048,512]{1,0:T(8,128)(2,1)}) %all-gather.4.cloned.1.call-update) | async-done | bytes 2097168 | tf_op jit(solution)/shard_map/all_gather | solution.py:222
  82.3 0.0 all-to-all-done
  82.3 0.0 all-gather.6.cloned.1.call-update
  82.3 3.7 %fusion.1 = (f32[512]{0:T(512)S(1)}, bf16[512,512]{0,1:T(8,128)(2,1)}) fusion(bf16[512,512]{0,1:T(8,128)(2,1)S(1)} %copy.8, f32[512]{0:T(512)S(1)} %broadcast_multiply_fusion, bf16[2048,512]{1,0:T(8,128)(2,1)S(1)} %bitcast.16, bf16[2048,512]{1,0:T(8,128)(2,1)} %all-gather.4.cloned.1.call-done.after_ref), kind=kOutput, calls=%fused_computation.3 | convolution fusion | flops 1075052032 | bytes 5246976 | tf_op jit(solution)/shard_map/dot_general | solution.py:258
  86.0 9.6 %all-to-all-start.1 = ((bf16[32,16,512]{2,1,0:T(8,128)(2,1)}), bf16[32,16,512]{2,1,0:T(8,128)(2,1)S(1)}, u32[]{:S(2)}, u32[]{:S(2)}) async-start(bf16[32,16,512]{2,1,0:T(8,128)(2,1)} %bitcast.4), calls=%async_computation.1 | async-start | bytes 1048576 | tf_op jit(solution)/shard_map/all_to_all | solution.py:263
  95.6 16.6 %all-to-all-done.1 = bf16[32,16,512]{2,1,0:T(8,128)(2,1)S(1)} async-done(((bf16[32,16,512]{2,1,0:T(8,128)(2,1)}), bf16[32,16,512]{2,1,0:T(8,128)(2,1)S(1)}, u32[]{:S(2)}, u32[]{:S(2)}) %all-to-all-start.1) | async-done | bytes 524320 | tf_op jit(solution)/shard_map/all_to_all | solution.py:263
  112.2 0.8 shard_map.70
  113.0 15.2 %all_to_all.26.parts_ref = f32[32,16,128]{2,1,0:T(8,128)S(1)} all-to-all(f32[32,16,128]{2,1,0:T(8,128)S(1)} %shard_map.70), channel_id=1, replica_groups=mesh['dp'=32,'fsdp'=16] {'dp'}, dimensions={0} | all-to-all | bytes 524288 | tf_op jit(solution)/shard_map/all_to_all | solution.py:271
  128.2 0.3 shard_map.71
  128.5 19.4 %all_to_all.27.packed_ref = f32[16,16,128]{2,1,0:T(8,128)S(1)} all-to-all(f32[16,16,128]{2,1,0:T(8,128)S(1)} %shard_map.71), channel_id=1, replica_groups=mesh['dp'=32,'fsdp'=16] {'fsdp'}, dimensions={0} | all-to-all | bytes 262144 | tf_op jit(solution)/shard_map/all_to_all | solution.py:275
  147.9 1.6 shard_map.72
  149.5 0.0 all-gather.6.cloned.1.call-done
  149.5 6.4 %shard_map.69 = bf16[128,8192]{1,0:T(8,128)(2,1)} custom-call(bf16[128,8192]{1,0:T(8,128)(2,1)} %input_hbm.1, bf16[128,512]{1,0:T(8,128)(2,1)} %cotangent_hbm.1, bf16[16,512,512]{2,1,0:T(8,128)(2,1)} %bitcast.15, f32[128,128]{1,0:T(8,128)} %get-tuple-element.11.scale_hbm), custom_call_target="tpu_custom_call" | custom-call | flops 1073741824 | bytes 12582912 | tf_op jit(solution)/shard_map/pallas_call | solution.py:276
  (3 shorter events, 0.0 us)
Async XLA Ops:
  7.2 75.1 %all-gather.4.cloned.1.call-start = ((), (), s32[]{:S(2)}) async-start(), calls=%async_computation.4 | async-start | bytes 2228224 | tf_op jit(solution)/shard_map/all_gather | solution.py:222
  11.0 12.0 %copy-start = (bf16[512,512]{1,0:T(8,128)(2,1)S(1)}, bf16[512,512]{1,0:T(8,128)(2,1)}, u32[]{:S(2)}) copy-start(bf16[512,512]{1,0:T(8,128)(2,1)} %param.6) | copy-start | bytes 1572868
  11.0 12.2 %copy-start.1 = (f32[512]{0:T(512)S(1)}, f32[512]{0:T(512)}, u32[]{:S(2)}) copy-start(f32[512]{0:T(512)} %param.5) | copy-start | bytes 6148
  11.0 71.2 %all-to-all-start = ((bf16[16,128,512]{2,1,0:T(8,128)(2,1)}), bf16[16,128,512]{2,1,0:T(8,128)(2,1)S(1)}, u32[]{:S(2)}, u32[]{:S(2)}) async-start(bf16[16,128,512]{2,1,0:T(8,128)(2,1)} %get-tuple-element.9), calls=%async_computation | async-start | bytes 4194304 | tf_op jit(solution)/shard_map/all_to_all | solution.py:238
  23.0 126.5 %all-gather.6.cloned.1.call-start = ((), (), s32[]{:S(2)}) async-start(), calls=%async_computation.5 | async-start | bytes 8912896 | tf_op jit(solution)/shard_map/all_gather | solution.py:255
  86.0 26.2 %all-to-all-start.1 = ((bf16[32,16,512]{2,1,0:T(8,128)(2,1)}), bf16[32,16,512]{2,1,0:T(8,128)(2,1)S(1)}, u32[]{:S(2)}, u32[]{:S(2)}) async-start(bf16[32,16,512]{2,1,0:T(8,128)(2,1)} %bitcast.4), calls=%async_computation.1 | async-start | bytes 1048576 | tf_op jit(solution)/shard_map/all_to_all | solution.py:263
Sparse Core Ops, SparseCore 0:
  10.1 72.1 all-gather.3
  84.4 60.4 all-gather.5

commit v7 on v6

--- a/solution.py
+++ b/solution.py
@@ -13,6 +13,7 @@
 LANES = 128
 CHUNKS = 4
 PARAMS = pltpu.CompilerParams(vmem_limit_bytes=32 * 1024 * 1024)
+INPUT = pltpu.CompilerParams(vmem_limit_bytes=46 * 1024 * 1024)
 LARGE = pltpu.CompilerParams(vmem_limit_bytes=60 * 1024 * 1024)
 
 
@@ -139,18 +140,16 @@
 
 
 def input_kernel(
-    input_hbm,
+    input_ref,
     cotangent_hbm,
     weight_hbm,
     scale_hbm,
     out_hbm,
-    input_ref,
     cotangent_ref,
     weight_ref,
     scale_ref,
     hat_ref,
     out_ref,
-    input_sem,
     small_sem,
     weight_sem,
     out_sem,
@@ -165,24 +164,16 @@
     arriving = []
     for part in range(CHUNKS):
         at = pl.ds(part * chunk, chunk)
-        columns = pl.ds(part * chunk * width, chunk * width)
-        pair = [
-            pltpu.make_async_copy(weight_hbm.at[at], weight_ref.at[at], weight_sem.at[part]),
-            pltpu.make_async_copy(
-                input_hbm.at[:, columns], input_ref.at[:, columns], input_sem.at[part]
-            ),
-        ]
-        for copy in pair:
-            copy.start()
-        arriving.append(pair)
+        copy = pltpu.make_async_copy(weight_hbm.at[at], weight_ref.at[at], weight_sem.at[part])
+        copy.start()
+        arriving.append(copy)
     small[1].start()
     small[0].wait()
     cotangent = cotangent_ref[...]
     total = jnp.zeros((cotangent.shape[0], LANES), jnp.float32)
     for block in range(blocks):
         if block % chunk == 0:
-            for copy in arriving[block // chunk]:
-                copy.wait()
+            arriving[block // chunk].wait()
         columns = slice(block * width, (block + 1) * width)
         hat = jnp.dot(cotangent, weight_ref[block], preferred_element_type=jnp.float32).astype(
             jnp.bfloat16
@@ -275,22 +266,20 @@
     packed = lax.all_to_all(sent, "fsdp", split_axis=0, concat_axis=0, tiled=True)
     input_grad = pl.pallas_call(
         input_kernel,
-        in_specs=[hbm, hbm, hbm, hbm],
+        in_specs=[pl.BlockSpec(memory_space=pltpu.VMEM), hbm, hbm, hbm],
         out_specs=hbm,
         out_shape=jax.ShapeDtypeStruct((tokens, model), jnp.bfloat16),
         scratch_shapes=[
-            pltpu.VMEM((tokens, model), jnp.bfloat16),
             pltpu.VMEM((tokens, width), jnp.bfloat16),
             pltpu.VMEM((peers, width, own), jnp.bfloat16),
             pltpu.VMEM((tokens, LANES), jnp.float32),
             pltpu.VMEM((tokens, model), jnp.bfloat16),
             pltpu.VMEM((tokens, model), jnp.bfloat16),
-            pltpu.SemaphoreType.DMA((CHUNKS,)),
             pltpu.SemaphoreType.DMA((2,)),
             pltpu.SemaphoreType.DMA((CHUNKS,)),
             pltpu.SemaphoreType.DMA((CHUNKS,)),
         ],
-        compiler_params=LARGE,
+        compiler_params=INPUT,
         cost_estimate=pl.CostEstimate(
             flops=2 * tokens * model * width, bytes_accessed=2 * model * (width + 2 * tokens), transcendentals=0
         ),

time: 163 us -> 163 us (level)
  no operation moved by 1% of the time
where the time goes in v7:
time: 163 us; the launch traced here: 162 us
  waiting for transfers between devices  75.4 us (46%)
  blocking collectives  34.4 us (21%)
  starting transfers between devices  21.8 us (13%)
  between operations  14.1 us (9%)
  Pallas kernels  11.9 us (7%)
  matrix products  3.72 us (2%)
    all_gather x1, waiting for transfers between devices, body(): cotangent = lax.all_gather(value_cotangent, 'fsdp', axis=0, tiled=True)  58.1 us
    all_to_all x1, blocking collectives, body(): lax.all_to_all(sent, 'fsdp', split_axis=0, concat_axis=0, tiled=True)  19.2 us
    all_to_all x1, waiting for transfers between devices, body(): lax.all_to_all(grad_w, 'dp', split_axis=0, concat_axis=0, tiled=True)  16.6 us
    all_to_all x1, blocking collectives, body(): parts = lax.all_to_all(sent, 'dp', split_axis=0, concat_axis=0, tiled=True)  15.2 us
    all_to_all x1, starting transfers between devices, body(): lax.all_to_all(blocks, 'fsdp', split_axis=0, concat_axis=0, tiled=True)  12 us
    all_to_all x1, starting transfers between devices, body(): lax.all_to_all(grad_w, 'dp', split_axis=0, concat_axis=0, tiled=True)  9.73 us
    pallas_call x1, Pallas kernels, body(): pl.pallas_call(input_kernel, in_specs=[pl.BlockSpec(memory_space=pltpu.VM...  6.07 us
    dot_general x1, matrix products, body(): lax.dot_general(cotangent, columns, (((0,), (0,)), ((), ())), preferred_e...  3.72 us
  transfers between devices with their start and end apart: 4, of which 2 were waited for; matrix products, arithmetic and copies ran while one was open for 3% of the time, Pallas kernels for 4%

profile of v7, /device:TPU:1, one launch (start us, length us, event | category | flops | bytes accessed | tf_op | source)
XLA Modules:
  0.0 162.4 jit_solution(10486402864494704280)
XLA Ops:
  7.2 0.0 all-gather.4.cloned.1.call-start
  7.2 0.7 all-gather.4.cloned.1.call-update
  7.9 3.1 %shard_map.68 = (bf16[16,128,512]{2,1,0:T(8,128)(2,1)}, f32[128,128]{1,0:T(8,128)}) custom-call(bf16[128,8192]{1,0:T(8,128)(2,1)} %input_ref.3), custom_call_target="tpu_custom_call" | custom-call | tf_op jit(solution)/shard_map/pallas_call | solution.py:215
  11.0 0.0 copy-start.3
  11.0 0.0 copy-start.4
  11.0 12.0 %all-to-all-start = ((bf16[16,128,512]{2,1,0:T(8,128)(2,1)}), bf16[16,128,512]{2,1,0:T(8,128)(2,1)S(1)}, u32[]{:S(2)}, u32[]{:S(2)}) async-start(bf16[16,128,512]{2,1,0:T(8,128)(2,1)} %get-tuple-element.9), calls=%async_computation | async-start | bytes 4194304 | tf_op jit(solution)/shard_map/all_to_all | solution.py:229
  23.0 0.0 all-gather.6.cloned.1.call-start
  23.1 0.0 copy-done.3
  23.1 0.2 copy.8
  23.3 0.0 copy-done.4
  23.3 0.9 fusion.2.value_ref
  24.2 58.1 %all-gather.4.cloned.1.call-done.after_ref = bf16[2048,512]{1,0:T(8,128)(2,1)} async-done(((bf16[128,512]{1,0:T(8,128)(2,1)}), bf16[2048,512]{1,0:T(8,128)(2,1)}) %all-gather.4.cloned.1.call-update) | async-done | bytes 2097168 | tf_op jit(solution)/shard_map/all_gather | solution.py:213
  82.3 0.0 all-to-all-done
  82.3 0.0 all-gather.6.cloned.1.call-update
  82.3 3.7 %fusion.1 = (f32[512]{0:T(512)S(1)}, bf16[512,512]{0,1:T(8,128)(2,1)}) fusion(bf16[512,512]{0,1:T(8,128)(2,1)S(1)} %copy.8, f32[512]{0:T(512)S(1)} %broadcast_multiply_fusion, bf16[2048,512]{1,0:T(8,128)(2,1)S(1)} %bitcast.16, bf16[2048,512]{1,0:T(8,128)(2,1)} %all-gather.4.cloned.1.call-done.after_ref), kind=kOutput, calls=%fused_computation.3 | convolution fusion | flops 1075052032 | bytes 5246976 | tf_op jit(solution)/shard_map/dot_general | solution.py:249
  86.0 0.0 copy-start
  86.0 0.0 copy-start.1
  86.0 0.0 copy-start.2
  86.0 9.7 %all-to-all-start.1 = ((bf16[32,16,512]{2,1,0:T(8,128)(2,1)}), bf16[32,16,512]{2,1,0:T(8,128)(2,1)S(1)}, u32[]{:S(2)}, u32[]{:S(2)}) async-start(bf16[32,16,512]{2,1,0:T(8,128)(2,1)} %bitcast.4), calls=%async_computation.1 | async-start | bytes 1048576 | tf_op jit(solution)/shard_map/all_to_all | solution.py:254
  95.8 16.6 %all-to-all-done.1 = bf16[32,16,512]{2,1,0:T(8,128)(2,1)S(1)} async-done(((bf16[32,16,512]{2,1,0:T(8,128)(2,1)}), bf16[32,16,512]{2,1,0:T(8,128)(2,1)S(1)}, u32[]{:S(2)}, u32[]{:S(2)}) %all-to-all-start.1) | async-done | bytes 524320 | tf_op jit(solution)/shard_map/all_to_all | solution.py:254
  112.4 0.8 shard_map.70
  113.2 15.2 %all_to_all.26.parts_ref = f32[32,16,128]{2,1,0:T(8,128)S(1)} all-to-all(f32[32,16,128]{2,1,0:T(8,128)S(1)} %shard_map.70), channel_id=1, replica_groups=mesh['dp'=32,'fsdp'=16] {'dp'}, dimensions={0} | all-to-all | bytes 524288 | tf_op jit(solution)/shard_map/all_to_all | solution.py:262
  128.3 0.3 shard_map.71
  128.6 19.2 %all_to_all.27.packed_ref = f32[16,16,128]{2,1,0:T(8,128)S(1)} all-to-all(f32[16,16,128]{2,1,0:T(8,128)S(1)} %shard_map.71), channel_id=1, replica_groups=mesh['dp'=32,'fsdp'=16] {'fsdp'}, dimensions={0} | all-to-all | bytes 262144 | tf_op jit(solution)/shard_map/all_to_all | solution.py:266
  147.8 1.6 shard_map.72
  149.4 0.0 all-gather.6.cloned.1.call-done
  149.4 0.0 copy-done
  149.5 0.0 copy-done.1
  149.5 0.0 copy-done.2
  149.5 6.1 %shard_map.69 = bf16[128,8192]{1,0:T(8,128)(2,1)} custom-call(bf16[128,8192]{1,0:T(8,128)(2,1)S(1)} %copy-done, bf16[128,512]{1,0:T(8,128)(2,1)S(1)} %copy-done.1, bf16[16,512,512]{2,1,0:T(8,128)(2,1)} %bitcast.15, f32[128,128]{1,0:T(8,128)S(1)} %copy-done.2), custom_call_target="tpu_custom_call" | custom-call | flops 1073741824 | bytes 12582912 | tf_op jit(solution)/shard_map/pallas_call | solution.py:267
  (3 shorter events, 0.0 us)
Async XLA Ops:
  7.2 75.1 %all-gather.4.cloned.1.call-start = ((), (), s32[]{:S(2)}) async-start(), calls=%async_computation.4 | async-start | bytes 2228224 | tf_op jit(solution)/shard_map/all_gather | solution.py:213
  11.0 12.0 %copy-start.3 = (bf16[512,512]{1,0:T(8,128)(2,1)S(1)}, bf16[512,512]{1,0:T(8,128)(2,1)}, u32[]{:S(2)}) copy-start(bf16[512,512]{1,0:T(8,128)(2,1)} %param.6) | copy-start | bytes 1572868
  11.0 12.2 %copy-start.4 = (f32[512]{0:T(512)S(1)}, f32[512]{0:T(512)}, u32[]{:S(2)}) copy-start(f32[512]{0:T(512)} %param.5) | copy-start | bytes 6148
  11.0 71.2 %all-to-all-start = ((bf16[16,128,512]{2,1,0:T(8,128)(2,1)}), bf16[16,128,512]{2,1,0:T(8,128)(2,1)S(1)}, u32[]{:S(2)}, u32[]{:S(2)}) async-start(bf16[16,128,512]{2,1,0:T(8,128)(2,1)} %get-tuple-element.9), calls=%async_computation | async-start | bytes 4194304 | tf_op jit(solution)/shard_map/all_to_all | solution.py:229
  23.0 126.4 %all-gather.6.cloned.1.call-start = ((), (), s32[]{:S(2)}) async-start(), calls=%async_computation.5 | async-start | bytes 8912896 | tf_op jit(solution)/shard_map/all_gather | solution.py:246
  86.0 63.4 %copy-start = (bf16[128,8192]{1,0:T(8,128)(2,1)S(1)}, bf16[128,8192]{1,0:T(8,128)(2,1)}, u32[]{:S(2)}) copy-start(bf16[128,8192]{1,0:T(8,128)(2,1)} %input_ref.3) | copy-start | bytes 6291460
  86.0 63.4 %copy-start.1 = (bf16[128,512]{1,0:T(8,128)(2,1)S(1)}, bf16[128,512]{1,0:T(8,128)(2,1)}, u32[]{:S(2)}) copy-start(bf16[128,512]{1,0:T(8,128)(2,1)} %cotangent_hbm.1) | copy-start | bytes 393220
  86.0 63.4 %copy-start.2 = (f32[128,128]{1,0:T(8,128)S(1)}, f32[128,128]{1,0:T(8,128)}, u32[]{:S(2)}) copy-start(f32[128,128]{1,0:T(8,128)} %get-tuple-element.11.scale_hbm) | copy-start | bytes 196612
  86.0 26.3 %all-to-all-start.1 = ((bf16[32,16,512]{2,1,0:T(8,128)(2,1)}), bf16[32,16,512]{2,1,0:T(8,128)(2,1)S(1)}, u32[]{:S(2)}, u32[]{:S(2)}) async-start(bf16[32,16,512]{2,1,0:T(8,128)(2,1)} %bitcast.4), calls=%async_computation.1 | async-start | bytes 1048576 | tf_op jit(solution)/shard_map/all_to_all | solution.py:254
Sparse Core Ops, SparseCore 0:
  10.1 72.1 all-gather.3
  84.4 60.2 all-gather.5
